TPU v7x, 512 devices: a whole 4x8x8 slice. The times are simulated.
512 devices in a mesh: row: 32 (over z, y_hi, core), col: 16 (over x, y_lo).
Axes of the slice: x: 4, y: 8 (y_hi: 2, y_lo: 4; y = y_hi * 4 + y_lo), z: 8, core: 2. Of those that a mesh axis runs over, the one named last changes fastest.
Arguments:
- raw: bfloat16 [256, 4096, 512], P(None, ('row', 'col')), may hold values from -40 to 40
Outputs:
- stack: bfloat16 [2, 16, 4096, 4096], P(None, None, 'row', 'col')
All inputs are finite; a program needn't handle non-finite values.
Results may differ from a plain program's by a relative error of at most 0.0054.
Values may be sent and summed in bfloat16 or wider, within the bound.
No kernel may reach another device: no remote copies, remote signals or barrier semaphores. Data moves between devices by JAX's collectives and lax.ppermute only.
A program may use at most 64 MiB of HBM per device.

v0:
```python
import math

import jax
import jax.numpy as jnp
from jax import lax
from jax.sharding import PartitionSpec as P

WINDOWS = 256
BINS = 16
LOW_BIN = 24
SPAN = 65


def broadcast(value, axis, root):
    mine = lax.axis_index(axis) == root
    return lax.psum(jnp.where(mine, value, jnp.zeros_like(value)), axis)


def whiten_local(raw):
    windows_here, count, length = raw.shape
    steps = jnp.arange(length)
    running = (jnp.abs(steps[:, None] - steps[None, :]) <= SPAN // 2).astype(jnp.bfloat16)
    flat = raw.reshape(-1, length)
    magnitude = jnp.dot(jnp.abs(flat), running, preferred_element_type=jnp.float32) / SPAN
    balanced = flat.astype(jnp.float32) / (magnitude + 1e-06)
    freqs = LOW_BIN + jnp.arange(BINS)
    angles = (steps[:, None] * freqs[None, :] % length).astype(jnp.float32) * (
        2.0 * math.pi / length
    )
    dft_table = jnp.concatenate([jnp.cos(angles), -jnp.sin(angles)], axis=1)
    spectrum = jnp.dot(balanced, dft_table, precision=lax.Precision.HIGHEST)
    spec_real = spectrum[:, :BINS]
    spec_imag = spectrum[:, BINS:]
    energy = spec_real * spec_real + spec_imag * spec_imag
    level = jnp.mean(energy, axis=1, keepdims=True)
    factor = lax.rsqrt(energy + 0.25 * level + 1.0)
    whitened = jnp.stack([spec_real * factor, spec_imag * factor]).astype(jnp.bfloat16)
    return whitened.reshape(2, windows_here, count, BINS).transpose(2, 0, 3, 1)


def cross_tile(left_block, right_block):
    left_real = left_block[:, 0]
    left_imag = left_block[:, 1]
    right_real = right_block[:, 0]
    right_imag = right_block[:, 1]
    cross_real = jnp.einsum(
        "ibw,jbw->bij", left_real, right_real, preferred_element_type=jnp.float32
    )
    cross_real = cross_real + jnp.einsum(
        "ibw,jbw->bij", left_imag, right_imag, preferred_element_type=jnp.float32
    )
    cross_imag = jnp.einsum(
        "ibw,jbw->bij", left_imag, right_real, preferred_element_type=jnp.float32
    )
    cross_imag = cross_imag - jnp.einsum(
        "ibw,jbw->bij", left_real, right_imag, preferred_element_type=jnp.float32
    )
    return (cross_real, cross_imag)


def on_device(raw):
    whitened = whiten_local(raw)
    fan_factor = lax.axis_size("row") // lax.axis_size("col")
    column_index = lax.axis_index("col")
    row_block = lax.all_gather(whitened, "col", axis=0, tiled=True)
    pieces = []
    for portion_index in range(fan_factor):
        source = fan_factor * column_index + portion_index
        pieces.append(broadcast(row_block, "row", source))
    column_block = jnp.concatenate(pieces, axis=0)
    total_real, total_imag = cross_tile(row_block, column_block)
    return (jnp.stack([total_real, total_imag]) / WINDOWS).astype(jnp.bfloat16)


def solution(mesh):
    return jax.shard_map(
        on_device,
        mesh=mesh,
        in_specs=(P(None, ("row", "col"), None),),
        out_specs=P(None, None, "row", "col"),
        check_vma=False,
    )
```

profile of v0, /device:TPU:10, one launch (start us, length us, event | category | flops | bytes accessed | tf_op | source)
XLA Modules:
  0.0 536.3 jit_solution(9364918310832868693)
XLA Ops:
  6.5 4.3 bitcast_convert_fusion
  10.8 3.3 fusion.2
  14.1 0.2 fusion.23
  14.3 5.5 %copy.13 = f32[2048,512]{0,1:T(8,128)} copy(f32[2048,512]{1,0:T(8,128)} %bitcast_convert_fusion) | data formatting | bytes 8388608 | tf_op jit(solution)/shard_map/convert_element_type | solution.py:25
  19.8 6.6 %fusion.1 = f32[2048,32]{0,1:T(8,128)S(1)} fusion(f32[2048,512]{0,1:T(8,128)} %copy.13, f32[512,2048]{1,0:T(8,128)} %fusion.2, f32[512,16]{0,1:T(8,128)S(1)} %get-tuple-element.12, f32[512,16]{0,1:T(8,128)S(1)} %get-tuple-element.11), kind=kOutput, calls=%fused_computation.3 | convolution fusion | flops 405815296 | bytes 8716288 | tf_op jit(solution)/shard_map/dot_general | solution.py:31
  26.5 0.3 copy.14
  26.8 0.4 copy.16
  27.1 0.3 copy.15
  27.4 0.4 copy.17
  27.8 0.7 maximum_bitcast_fusion
  28.5 0.0 all-gather.2.cloned.1.call-update
  28.5 0.0 all-reduce.3.cloned.1.call-start
  28.5 91.6 %all-gather.2.cloned.1.call-done = bf16[128,2,16,256]{3,0,2,1:T(8,128)(2,1)} async-done(((bf16[8,2,16,256]{3,0,2,1:T(8,128)(2,1)}), bf16[128,2,16,256]{3,0,2,1:T(8,128)(2,1)}) %all-gather.2.cloned.1.call-update) | async-done | bytes 2097168 | tf_op jit(solution)/shard_map/all_gather | solution.py:65
  120.1 3.9 broadcast_select_fusion
  124.0 396.4 %all-reduce.3.cloned.1.call-done = (bf16[128,2,16,256]{3,0,2,1:T(8,128)(2,1)}, bf16[128,2,16,256]{3,0,2,1:T(8,128)(2,1)}) async-done(((bf16[128,2,16,256]{3,0,2,1:T(8,128)(2,1)}, bf16[128,2,16,256]{3,0,2,1:T(8,128)(2,1)}), (bf16[128,2,16,256]{3,0,2,1:T(8,128)(2,1)}, bf16[128,2,16,256]{3,0,2,1:T(8,128)(2,1)})) %all-reduce.3.cloned.1.call-update) | async-done | bytes 4194320 | tf_op jit(solution)/shard_map/psum | solution.py:16
  520.5 1.9 constant_dynamic-update-slice_fusion.1
  522.4 0.3 copy-done.2
  522.7 0.2 constant_dynamic-update-slice_fusion
  522.9 1.4 copy-done
  524.3 0.8 fusion.8
  525.1 0.8 fusion.7
  525.9 0.8 add_bitcast_fusion
  526.8 0.8 subtract_bitcast_fusion
  527.6 1.9 fusion
  (10 shorter events, 0.1 us)
Async XLA Ops:
  6.5 113.6 %all-gather.2.cloned.1.call-start = ((), (), s32[]{:S(2)}) async-start(), calls=%async_computation | async-start | bytes 2228224 | tf_op jit(solution)/shard_map/all_gather | solution.py:65
  6.5 4.3 copy-start.1
  28.5 492.0 %all-reduce.3.cloned.1.call-start = ((), (), s32[]{:S(2)}) async-start(), calls=%async_computation.1 | async-start | bytes 8388608 | tf_op jit(solution)/shard_map/psum | solution.py:16
  520.5 2.2 copy-start.2
  522.7 1.6 copy-start
Sparse Core Ops, SparseCore 0:
  28.6 91.4 all-gather.1
  124.2 396.2 all-reduce.2
where the time goes:
time: 537 us; the launch traced here: 536 us
  waiting for transfers between devices  488 us (91%)
  between operations  13.5 us (3%)
  matrix products  13.1 us (2%)
  other arithmetic  11 us (2%)
  local copies, waits for them, and re-layouts  10.5 us (2%)
    psum x1, waiting for transfers between devices, broadcast(): return lax.psum(jnp.where(mine, value, jnp.zeros_like(value)), axis)  396 us
    all_gather x1, waiting for transfers between devices, on_device(): row_block = lax.all_gather(whitened, 'col', axis=0, tiled=True)  91.6 us
  transfers between devices with their start and end apart: 2, of which 2 were waited for; matrix products, arithmetic and copies ran while one was open for 0% of the time, Pallas kernels for 0%

commit v1 on v0

v1 whole, which is shorter than its diff:
```python
import math

import jax
import jax.numpy as jnp
import numpy as np
from jax import lax
from jax.experimental import pallas as pl
from jax.experimental.pallas import tpu as pltpu
from jax.sharding import Mesh, PartitionSpec as P

WINDOWS = 256
SAMPLES = 512
BINS = 16
LOW_BIN = 24
SPAN = 65
AXES = ("z", "yh", "core", "x", "yl")
SIZES = {"z": 8, "yh": 2, "core": 2, "x": 4, "yl": 4}
STEPS = 2
PER_STEP = WINDOWS // STEPS


def tables():
    steps = np.arange(SAMPLES)
    band = (np.abs(steps[:, None] - steps[None, :]) <= SPAN // 2).astype(np.float32)
    freqs = LOW_BIN + np.arange(BINS)
    angles = (steps[None, :] * freqs[:, None] % SAMPLES) * (2.0 * math.pi / SAMPLES)
    dft = np.concatenate([np.cos(angles), -np.sin(angles)], axis=0).astype(np.float32)
    high = dft.astype(jnp.bfloat16)
    low = (dft - high.astype(np.float32)).astype(jnp.bfloat16)
    return band.astype(jnp.bfloat16), np.concatenate([high, low], axis=0)


def nt_dot(left, right):
    return lax.dot_general(
        left, right, (((1,), (1,)), ((), ())), preferred_element_type=jnp.float32
    )


def whiten_kernel(raw_ref, band_ref, dft_ref, out_ref, balanced_ref, white_ref):
    flat = raw_ref[...]
    total = jnp.dot(jnp.abs(flat), band_ref[...], preferred_element_type=jnp.float32)
    balanced = flat.astype(jnp.float32) / (total * (1.0 / SPAN) + 1e-06)
    for part in range(4):
        balanced_ref[part] = balanced[:, part * 128 : (part + 1) * 128]
    dft = dft_ref[...]
    for channel in range(8):
        balanced = jnp.concatenate(
            [balanced_ref[part, pl.ds(channel, PER_STEP, stride=8), :] for part in range(4)],
            axis=1,
        )
        high = balanced.astype(jnp.bfloat16)
        low = (balanced - high.astype(jnp.float32)).astype(jnp.bfloat16)
        wide = nt_dot(dft, high)
        spectrum = wide[: 2 * BINS] + (wide[2 * BINS :] + nt_dot(dft[: 2 * BINS], low))
        real = spectrum[:BINS]
        imag = spectrum[BINS:]
        energy = real * real + imag * imag
        level = jnp.mean(energy, axis=0, keepdims=True)
        factor = lax.rsqrt(energy + 0.25 * level + 1.0)
        white_ref[:, channel, :PER_STEP] = real * factor
        white_ref[:, channel, PER_STEP:] = imag * factor
    out_ref[...] = white_ref[...].astype(jnp.bfloat16)


def whiten(raw):
    band, dft = tables()
    rows = PER_STEP * 8
    return pl.pallas_call(
        whiten_kernel,
        grid=(STEPS,),
        in_specs=[
            pl.BlockSpec((rows, SAMPLES), lambda g: (g, 0)),
            pl.BlockSpec((SAMPLES, SAMPLES), lambda g: (0, 0)),
            pl.BlockSpec((4 * BINS, SAMPLES), lambda g: (0, 0)),
        ],
        out_specs=pl.BlockSpec((BINS, 8, 2 * PER_STEP), lambda g: (0, 0, g)),
        out_shape=jax.ShapeDtypeStruct((BINS, 8, 2 * WINDOWS), jnp.bfloat16),
        scratch_shapes=[
            pltpu.VMEM((4, rows, 128), jnp.float32),
            pltpu.VMEM((BINS, 8, 2 * PER_STEP), jnp.float32),
        ],
        compiler_params=pltpu.CompilerParams(vmem_limit_bytes=32 << 20),
        cost_estimate=pl.CostEstimate(
            flops=3_000_000_000, bytes_accessed=3 << 20, transcendentals=1 << 20
        ),
        name="whiten",
    )(raw.reshape(WINDOWS * 8, SAMPLES), jnp.asarray(band), jnp.asarray(dft))


def cross_kernel(place_ref, rows_ref, *refs):
    pieces = refs[:8]
    out_ref, left_ref, right_ref, tile_ref, row_sem, piece_sem, out_sem = refs[8:]
    row_copy = pltpu.make_async_copy(rows_ref, left_ref, row_sem)
    row_copy.start()
    copies = []
    for piece in pieces:
        for slot in range(piece.shape[0]):
            k = len(copies)
            copy = pltpu.make_async_copy(
                piece.at[slot], right_ref.at[place_ref[k]], piece_sem.at[k]
            )
            copy.start()
            copies.append(copy)
    row_copy.wait()
    for copy in copies:
        copy.wait()
    half = PER_STEP
    outs = []
    for b in range(BINS):
        left = left_ref[:, b].astype(jnp.float32).reshape(128, 2 * WINDOWS)
        right = right_ref[:, b].astype(jnp.float32).reshape(256, 2 * WINDOWS)
        right = right.astype(jnp.bfloat16)
        turned = []
        for g in range(STEPS):
            turned.append(left[:, (2 * g + 1) * half : (2 * g + 2) * half])
            turned.append(-left[:, 2 * g * half : (2 * g + 1) * half])
        turned = jnp.concatenate(turned, axis=1).astype(jnp.bfloat16)
        left = left.astype(jnp.bfloat16)
        tile_ref[0, b] = (nt_dot(left, right) * (1.0 / WINDOWS)).astype(jnp.bfloat16)
        tile_ref[1, b] = (nt_dot(turned, right) * (1.0 / WINDOWS)).astype(jnp.bfloat16)
        if b % 4 == 3:
            part = pl.ds(b - 3, 4)
            copy = pltpu.make_async_copy(
                tile_ref.at[:, part], out_ref.at[:, part], out_sem.at[b // 4]
            )
            copy.start()
            outs.append(copy)
    for copy in outs:
        copy.wait()


def cross(places, rows, pieces):
    block = (BINS, 8, 2 * WINDOWS)
    out = (2, BINS, 128, 256)
    anywhere = pl.BlockSpec(memory_space=pl.ANY)
    return pl.pallas_call(
        cross_kernel,
        in_specs=[pl.BlockSpec(memory_space=pltpu.SMEM)] + [anywhere] * 9,
        out_specs=anywhere,
        out_shape=jax.ShapeDtypeStruct(out, jnp.bfloat16),
        scratch_shapes=[
            pltpu.VMEM((16,) + block, jnp.bfloat16),
            pltpu.VMEM((32,) + block, jnp.bfloat16),
            pltpu.VMEM(out, jnp.bfloat16),
            pltpu.SemaphoreType.DMA,
            pltpu.SemaphoreType.DMA((32,)),
            pltpu.SemaphoreType.DMA((4,)),
        ],
        compiler_params=pltpu.CompilerParams(vmem_limit_bytes=48 << 20),
        cost_estimate=pl.CostEstimate(
            flops=1_100_000_000, bytes_accessed=8 << 20, transcendentals=0
        ),
        name="cross",
    )(places, rows, *pieces)


def flat(z, yh, core, x, yl):
    return (((z * 2 + yh) * 2 + core) * 4 + x) * 4 + yl


def everyone():
    for index in np.ndindex(*(SIZES[a] for a in AXES)):
        yield index


def spread_pairs(turn):
    pairs = []
    for z, yh, core, x, yl in everyone():
        home = z * 2 + yh
        target = (turn + x) % 4
        layer = (x + yl + z) % 4 + 4 * (target // 2)
        pairs.append((flat(z, yh, core, x, yl), flat(layer, target % 2, core, home // 4, home % 4)))
    return pairs


def ring(value, axis, by):
    n = SIZES[axis]
    return lax.ppermute(value, axis, [(i, (i + by) % n) for i in range(n)])


def swap(value):
    return ring(value, "core", 1)


def places_here():
    table = []
    for z, yh, core, x, yl in everyone():
        home_z = (x * 4 + yl) // 2
        row = []
        for side in (core, 1 - core):
            for away, slots in ((0, 4), (-1, 4), (1, 4), (-2, 2), (2, 2)):
                layer = (z + away) % 8
                for slot in range(slots):
                    from_x = (2 * (layer // 4) + yh - slot) % 4
                    row.append(side * 16 + from_x * 4 + (layer - from_x - home_z) % 4)
        assert sorted(row) == list(range(32))
        table.append(row)
    table = jnp.asarray(np.array(table, np.int32))
    return lax.dynamic_index_in_dim(table, lax.axis_index(AXES), keepdims=False)


def on_device(raw):
    white = whiten(raw)
    here = jnp.stack([lax.ppermute(white, AXES, spread_pairs(turn)) for turn in range(4)])
    rows = lax.all_gather(lax.all_gather(white, "yl"), "x")
    rows = rows.reshape((16,) + white.shape)
    below = ring(here, "z", 1)
    above = ring(here, "z", -1)
    far = jnp.concatenate([ring(below[:2], "z", 1), ring(above[:2], "z", -1)])
    mine = [here, below, above, far]
    pieces = mine + [swap(piece) for piece in mine]
    return cross(places_here(), rows, pieces)


def solution(mesh):
    split = Mesh(mesh.devices.reshape([SIZES[a] for a in AXES]), AXES)
    return jax.shard_map(
        on_device,
        mesh=split,
        in_specs=(P(None, AXES, None),),
        out_specs=P(None, None, ("z", "yh", "core"), ("x", "yl")),
        check_vma=False,
    )
```

time: 537 us -> 124 us (0.23)
  the two profiles are of different devices: /device:TPU:10 before, /device:TPU:193 now
where the time goes in v1:
time: 124 us
  starting transfers between devices  52 us (42%)
  waiting for transfers between devices  25.8 us (21%)
  blocking collectives  14.8 us (12%)
  between operations  13.6 us (11%)
  Pallas kernels  13.3 us (11%)
  local copies, waits for them, and re-layouts  4.24 us (3%)
    ppermute x8, starting transfers between devices, ring(): return lax.ppermute(value, axis, [(i, (i + by) % n) for i in range(n)])  32 us
    ppermute x4, starting transfers between devices, on_device(): lax.ppermute(white, AXES, spread_pairs(turn))  20 us
    ppermute x4, waiting for transfers between devices, on_device(): lax.ppermute(white, AXES, spread_pairs(turn))  17.4 us
    all_gather x1, blocking collectives, on_device(): rows = lax.all_gather(lax.all_gather(white, 'yl'), 'x')  14.8 us
    pallas_call x1, Pallas kernels, cross(): pl.pallas_call(cross_kernel, in_specs=[pl.BlockSpec(memory_space=pltpu.SM...  9.66 us
    ppermute x8, waiting for transfers between devices, ring(): return lax.ppermute(value, axis, [(i, (i + by) % n) for i in range(n)])  8.38 us
    pallas_call x1, Pallas kernels, whiten(): pl.pallas_call(whiten_kernel, grid=(STEPS,), in_specs=[pl.BlockSpec((rows...  3.68 us
    unnamed x7, local copies, waits for them, and re-layouts  3.49 us
  transfers between devices with their start and end apart: 13, of which 4 were waited for; matrix products, arithmetic and copies ran while one was open for 1% of the time, Pallas kernels for 0%

profile of v1, /device:TPU:193, one launch (start us, length us, event | category | flops | bytes accessed | tf_op | source)
XLA Modules:
  0.0 123.9 jit_solution(9756363675789338466)
XLA Ops:
  6.5 1.6 %copy-done = bf16[256,8,512]{2,1,0:T(8,128)(2,1)S(1)} copy-done((bf16[256,8,512]{2,1,0:T(8,128)(2,1)S(1)}, bf16[256,8,512]{2,1,0:T(8,128)(2,1)}, u32[]{:S(2)}) %copy-start) | copy-done | bytes 2097176
  8.1 1.0 copy-done.1
  9.2 0.8 copy-done.2
  10.0 3.7 %whiten.1 = bf16[16,8,512]{2,1,0:T(8,128)(2,1)S(1)} custom-call(bf16[2048,512]{1,0:T(8,128)(2,1)S(1)} %bitcast.8, bf16[512,512]{1,0:T(8,128)(2,1)S(1)} %copy-done.1, bf16[64,512]{1,0:T(8,128)(2,1)S(1)} %copy-done.2), custom_call_target="tpu_custom_call" | custom-call | flops 3000000000 | bytes 3145728 | tf_op jit(solution)/shard_map/whiten/pallas_call | solution.py:68
  13.7 14.8 %all-gather = bf16[64,8,512]{2,1,0:T(8,128)(2,1)} all-gather(bf16[16,8,512]{2,1,0:T(8,128)(2,1)S(1)} %whiten.1), channel_id=2, replica_groups=mesh['z'=8,'yh'=2,'core'=2,'x'=4,'yl'=4] {'yl'}, dimensions={0}, use_global_device_ids=true | all-gather | bytes 655360 | tf_op jit(solution)/shard_map/all_gather | solution.py:205
  28.5 10.6 %collective-permute-start.3 = (bf16[16,8,512]{2,1,0:T(8,128)(2,1)S(1)}, bf16[16,8,512]{2,1,0:T(8,128)(2,1)S(1)}, u32[]{:S(2)}, u32[]{:S(2)}) collective-permute-start(bf16[16,8,512]{2,1,0:T(8,128)(2,1)S(1)} %whiten.1), channel_id=1, source_target_pairs={{0,288},{1,352},{2,416},{3,480},{4,64},{5,128},{6,192},{7,0},{8,16... | collective-permute-start | bytes 393224 | tf_op jit(solution)/shard_map/ppermute | solution.py:204
  39.2 1.9 %collective-permute-start.2 = (bf16[16,8,512]{2,1,0:T(8,128)(2,1)S(1)}, bf16[16,8,512]{2,1,0:T(8,128)(2,1)S(1)}, u32[]{:S(2)}, u32[]{:S(2)}) collective-permute-start(bf16[16,8,512]{2,1,0:T(8,128)(2,1)S(1)} %whiten.1), channel_id=1, source_target_pairs={{0,256},{1,320},{2,384},{3,448},{4,352},{5,416},{6,480},{7,288},{8... | collective-permute-start | bytes 393224 | tf_op jit(solution)/shard_map/ppermute | solution.py:204
  41.1 2.7 %collective-permute-start.1 = (bf16[16,8,512]{2,1,0:T(8,128)(2,1)S(1)}, bf16[16,8,512]{2,1,0:T(8,128)(2,1)S(1)}, u32[]{:S(2)}, u32[]{:S(2)}) collective-permute-start(bf16[16,8,512]{2,1,0:T(8,128)(2,1)S(1)} %whiten.1), channel_id=1, source_target_pairs={{0,32},{1,96},{2,160},{3,224},{4,320},{5,384},{6,448},{7,256},{8,4... | collective-permute-start | bytes 393224 | tf_op jit(solution)/shard_map/ppermute | solution.py:204
  43.8 4.8 %collective-permute-start = (bf16[16,8,512]{2,1,0:T(8,128)(2,1)S(1)}, bf16[16,8,512]{2,1,0:T(8,128)(2,1)S(1)}, u32[]{:S(2)}, u32[]{:S(2)}) collective-permute-start(bf16[16,8,512]{2,1,0:T(8,128)(2,1)S(1)} %whiten.1), channel_id=1, source_target_pairs={{0,0},{1,64},{2,128},{3,192},{4,96},{5,160},{6,224},{7,32},{8,384}... | collective-permute-start | bytes 393224 | tf_op jit(solution)/shard_map/ppermute | solution.py:204
  48.6 5.6 %collective-permute-done.2 = bf16[16,8,512]{2,1,0:T(8,128)(2,1)S(1)} collective-permute-done((bf16[16,8,512]{2,1,0:T(8,128)(2,1)S(1)}, bf16[16,8,512]{2,1,0:T(8,128)(2,1)S(1)}, u32[]{:S(2)}, u32[]{:S(2)}) %collective-permute-start.2) | collective-permute-done | bytes 131104 | tf_op jit(solution)/shard_map/ppermute | solution.py:204
  54.2 11.8 %collective-permute-done.1 = bf16[16,8,512]{2,1,0:T(8,128)(2,1)S(1)} collective-permute-done((bf16[16,8,512]{2,1,0:T(8,128)(2,1)S(1)}, bf16[16,8,512]{2,1,0:T(8,128)(2,1)S(1)}, u32[]{:S(2)}, u32[]{:S(2)}) %collective-permute-start.1) | collective-permute-done | bytes 131104 | tf_op jit(solution)/shard_map/ppermute | solution.py:204
  66.0 0.1 pad_maximum_fusion.refs_0_
  66.1 10.4 %collective-permute-start.4 = (bf16[4,16,8,512]{3,2,1,0:T(8,128)(2,1)S(1)}, bf16[4,16,8,512]{3,2,1,0:T(8,128)(2,1)S(1)}, u32[]{:S(2)}, u32[]{:S(2)}) collective-permute-start(bf16[4,16,8,512]{3,2,1,0:T(8,128)(2,1)S(1)} %pad_maximum_fusion.refs_0_), channel_id=1, source_target_pairs={{0,64},{64,128},{128,192},{192,256},{256,320},{320,384},{384,448},... | collective-permute-start | bytes 1572872 | tf_op jit(solution)/shard_map/ppermute | solution.py:178
  76.5 1.9 %collective-permute-start.5 = (bf16[4,16,8,512]{3,2,1,0:T(8,128)(2,1)S(1)}, bf16[4,16,8,512]{3,2,1,0:T(8,128)(2,1)S(1)}, u32[]{:S(2)}, u32[]{:S(2)}) collective-permute-start(bf16[4,16,8,512]{3,2,1,0:T(8,128)(2,1)S(1)} %pad_maximum_fusion.refs_0_), channel_id=1, source_target_pairs={{0,448},{64,0},{128,64},{192,128},{256,192},{320,256},{384,320},{4... | collective-permute-start | bytes 1572872 | tf_op jit(solution)/shard_map/ppermute | solution.py:178
  78.4 7.4 %collective-permute-done.4.refs_1_ = bf16[4,16,8,512]{3,2,1,0:T(8,128)(2,1)S(1)} collective-permute-done((bf16[4,16,8,512]{3,2,1,0:T(8,128)(2,1)S(1)}, bf16[4,16,8,512]{3,2,1,0:T(8,128)(2,1)S(1)}, u32[]{:S(2)}, u32[]{:S(2)}) %collective-permute-start.4) | collective-permute-done | bytes 524320 | tf_op jit(solution)/shard_map/ppermute | solution.py:178
  85.9 5.3 %collective-permute-start.6 = (bf16[2,16,8,512]{3,2,1,0:T(8,128)(2,1)S(1)}, bf16[2,16,8,512]{3,2,1,0:T(8,128)(2,1)S(1)}, u32[]{:S(2)}, u32[]{:S(2)}) collective-permute-start(bf16[2,16,8,512]{3,2,1,0:T(8,128)(2,1)S(1)} %slice.8), channel_id=1, source_target_pairs={{0,64},{64,128},{128,192},{192,256},{256,320},{320,384},{384,448},... | collective-permute-start | bytes 786440 | tf_op jit(solution)/shard_map/ppermute | solution.py:178
  91.3 1.9 %collective-permute-start.7 = (bf16[2,16,8,512]{3,2,1,0:T(8,128)(2,1)S(1)}, bf16[2,16,8,512]{3,2,1,0:T(8,128)(2,1)S(1)}, u32[]{:S(2)}, u32[]{:S(2)}) collective-permute-start(bf16[2,16,8,512]{3,2,1,0:T(8,128)(2,1)S(1)} %slice.9), channel_id=1, source_target_pairs={{0,448},{64,0},{128,64},{192,128},{256,192},{320,256},{384,320},{4... | collective-permute-start | bytes 786440 | tf_op jit(solution)/shard_map/ppermute | solution.py:178
  93.2 4.9 %collective-permute-start.8 = (bf16[4,16,8,512]{3,2,1,0:T(8,128)(2,1)S(1)}, bf16[4,16,8,512]{3,2,1,0:T(8,128)(2,1)S(1)}, u32[]{:S(2)}, u32[]{:S(2)}) collective-permute-start(bf16[4,16,8,512]{3,2,1,0:T(8,128)(2,1)S(1)} %pad_maximum_fusion.refs_0_), channel_id=1, source_target_pairs={{0,16},{16,0},{1,17},{17,1},{2,18},{18,2},{3,19},{19,3},{4,20},{20... | collective-permute-start | bytes 1572872 | tf_op jit(solution)/shard_map/ppermute | solution.py:178
  98.1 1.9 %collective-permute-start.10 = (bf16[4,16,8,512]{3,2,1,0:T(8,128)(2,1)S(1)}, bf16[4,16,8,512]{3,2,1,0:T(8,128)(2,1)S(1)}, u32[]{:S(2)}, u32[]{:S(2)}) collective-permute-start(bf16[4,16,8,512]{3,2,1,0:T(8,128)(2,1)S(1)} %collective-permute-done.5.refs_2_), channel_id=1, source_target_pairs={{0,16},{16,0},{1,17},{17,1},{2,18},{18,2},{3,19},{19,3},{4,20},{20... | collective-permute-start | bytes 1572872 | tf_op jit(solution)/shard_map/ppermute | solution.py:178
  100.1 2.4 %collective-permute-start.9 = (bf16[4,16,8,512]{3,2,1,0:T(8,128)(2,1)S(1)}, bf16[4,16,8,512]{3,2,1,0:T(8,128)(2,1)}, u32[]{:S(2)}, u32[]{:S(2)}) collective-permute-start(bf16[4,16,8,512]{3,2,1,0:T(8,128)(2,1)S(1)} %collective-permute-done.4.refs_1_), channel_id=1, source_target_pairs={{0,16},{16,0},{1,17},{17,1},{2,18},{18,2},{3,19},{19,3},{4,20},{20... | collective-permute-start | bytes 1572872 | tf_op jit(solution)/shard_map/ppermute | solution.py:178
  102.5 3.1 %collective-permute-start.11 = (bf16[4,16,8,512]{3,2,1,0:T(8,128)(2,1)S(1)}, bf16[4,16,8,512]{3,2,1,0:T(8,128)(2,1)}, u32[]{:S(2)}, u32[]{:S(2)}) collective-permute-start(bf16[4,16,8,512]{3,2,1,0:T(8,128)(2,1)S(1)} %constant_dynamic-update-slice_fusion.refs_3_), channel_id=1, source_target_pairs={{0,16},{16,0},{1,17},{17,1},{2,18},{18,2},{3,19},{19,3},{4,20},{20... | collective-permute-start | bytes 1572872 | tf_op jit(solution)/shard_map/ppermute | solution.py:178
  105.7 0.7 dynamic-slice_bitcast_fusion.place_ref
  106.4 0.9 collective-permute-done.11.refs_7_
  107.3 9.7 %cross.1 = bf16[2,16,128,256]{3,2,1,0:T(8,128)(2,1)} custom-call(s32[32]{0:T(128)S(1)} %dynamic-slice_bitcast_fusion.place_ref, bf16[16,16,8,512]{3,2,1,0:T(8,128)(2,1)} %all-gather.4.cloned.1.call-done.rows_ref, bf16[4,16,8,512]{3,2,1,0:T(8,128)(2,1)S(1)} %pad_maximum_fusion.refs_0_, bf16[4,16,8,512]{3,2,1,0:T(8,128)(2,1)S(1)} %collective-permute-done.4.refs_1_, ...), custom_call_target="tpu_custom_call" | custom-call | flops 1100000000 | bytes 8388608 | tf_op jit(solution)/shard_map/cross/pallas_call | solution.py:136
  (18 shorter events, 0.1 us)
Async XLA Ops:
  6.5 100.8 %all-gather.4.cloned.1.call-start = ((), (), s32[]{:S(2)}) async-start(), calls=%async_computation | async-start | bytes 2621440 | tf_op jit(solution)/shard_map/all_gather | solution.py:205
  6.5 1.6 %copy-start = (bf16[256,8,512]{2,1,0:T(8,128)(2,1)S(1)}, bf16[256,8,512]{2,1,0:T(8,128)(2,1)}, u32[]{:S(2)}) copy-start(bf16[256,8,512]{2,1,0:T(8,128)(2,1)} %param.4) | copy-start | bytes 6291460
  8.1 1.0 copy-start.1
  9.2 0.8 copy-start.2
  28.5 20.1 %collective-permute-start.3 = (bf16[16,8,512]{2,1,0:T(8,128)(2,1)S(1)}, bf16[16,8,512]{2,1,0:T(8,128)(2,1)S(1)}, u32[]{:S(2)}, u32[]{:S(2)}) collective-permute-start(bf16[16,8,512]{2,1,0:T(8,128)(2,1)S(1)} %whiten.1), channel_id=1, source_target_pairs={{0,288},{1,352},{2,416},{3,480},{4,64},{5,128},{6,192},{7,0},{8,16... | collective-permute-start | bytes 393224 | tf_op jit(solution)/shard_map/ppermute | solution.py:204
  39.2 15.0 %collective-permute-start.2 = (bf16[16,8,512]{2,1,0:T(8,128)(2,1)S(1)}, bf16[16,8,512]{2,1,0:T(8,128)(2,1)S(1)}, u32[]{:S(2)}, u32[]{:S(2)}) collective-permute-start(bf16[16,8,512]{2,1,0:T(8,128)(2,1)S(1)} %whiten.1), channel_id=1, source_target_pairs={{0,256},{1,320},{2,384},{3,448},{4,352},{5,416},{6,480},{7,288},{8... | collective-permute-start | bytes 393224 | tf_op jit(solution)/shard_map/ppermute | solution.py:204
  41.1 24.9 %collective-permute-start.1 = (bf16[16,8,512]{2,1,0:T(8,128)(2,1)S(1)}, bf16[16,8,512]{2,1,0:T(8,128)(2,1)S(1)}, u32[]{:S(2)}, u32[]{:S(2)}) collective-permute-start(bf16[16,8,512]{2,1,0:T(8,128)(2,1)S(1)} %whiten.1), channel_id=1, source_target_pairs={{0,32},{1,96},{2,160},{3,224},{4,320},{5,384},{6,448},{7,256},{8,4... | collective-permute-start | bytes 393224 | tf_op jit(solution)/shard_map/ppermute | solution.py:204
  43.8 22.2 %collective-permute-start = (bf16[16,8,512]{2,1,0:T(8,128)(2,1)S(1)}, bf16[16,8,512]{2,1,0:T(8,128)(2,1)S(1)}, u32[]{:S(2)}, u32[]{:S(2)}) collective-permute-start(bf16[16,8,512]{2,1,0:T(8,128)(2,1)S(1)} %whiten.1), channel_id=1, source_target_pairs={{0,0},{1,64},{2,128},{3,192},{4,96},{5,160},{6,224},{7,32},{8,384}... | collective-permute-start | bytes 393224 | tf_op jit(solution)/shard_map/ppermute | solution.py:204
  66.1 19.8 %collective-permute-start.4 = (bf16[4,16,8,512]{3,2,1,0:T(8,128)(2,1)S(1)}, bf16[4,16,8,512]{3,2,1,0:T(8,128)(2,1)S(1)}, u32[]{:S(2)}, u32[]{:S(2)}) collective-permute-start(bf16[4,16,8,512]{3,2,1,0:T(8,128)(2,1)S(1)} %pad_maximum_fusion.refs_0_), channel_id=1, source_target_pairs={{0,64},{64,128},{128,192},{192,256},{256,320},{320,384},{384,448},... | collective-permute-start | bytes 1572872 | tf_op jit(solution)/shard_map/ppermute | solution.py:178
  76.5 14.7 %collective-permute-start.5 = (bf16[4,16,8,512]{3,2,1,0:T(8,128)(2,1)S(1)}, bf16[4,16,8,512]{3,2,1,0:T(8,128)(2,1)S(1)}, u32[]{:S(2)}, u32[]{:S(2)}) collective-permute-start(bf16[4,16,8,512]{3,2,1,0:T(8,128)(2,1)S(1)} %pad_maximum_fusion.refs_0_), channel_id=1, source_target_pairs={{0,448},{64,0},{128,64},{192,128},{256,192},{320,256},{384,320},{4... | collective-permute-start | bytes 1572872 | tf_op jit(solution)/shard_map/ppermute | solution.py:178
  85.9 16.6 %collective-permute-start.6 = (bf16[2,16,8,512]{3,2,1,0:T(8,128)(2,1)S(1)}, bf16[2,16,8,512]{3,2,1,0:T(8,128)(2,1)S(1)}, u32[]{:S(2)}, u32[]{:S(2)}) collective-permute-start(bf16[2,16,8,512]{3,2,1,0:T(8,128)(2,1)S(1)} %slice.8), channel_id=1, source_target_pairs={{0,64},{64,128},{128,192},{192,256},{256,320},{320,384},{384,448},... | collective-permute-start | bytes 786440 | tf_op jit(solution)/shard_map/ppermute | solution.py:178
  91.3 11.3 %collective-permute-start.7 = (bf16[2,16,8,512]{3,2,1,0:T(8,128)(2,1)S(1)}, bf16[2,16,8,512]{3,2,1,0:T(8,128)(2,1)S(1)}, u32[]{:S(2)}, u32[]{:S(2)}) collective-permute-start(bf16[2,16,8,512]{3,2,1,0:T(8,128)(2,1)S(1)} %slice.9), channel_id=1, source_target_pairs={{0,448},{64,0},{128,64},{192,128},{256,192},{320,256},{384,320},{4... | collective-permute-start | bytes 786440 | tf_op jit(solution)/shard_map/ppermute | solution.py:178
  93.2 13.2 %collective-permute-start.8 = (bf16[4,16,8,512]{3,2,1,0:T(8,128)(2,1)S(1)}, bf16[4,16,8,512]{3,2,1,0:T(8,128)(2,1)S(1)}, u32[]{:S(2)}, u32[]{:S(2)}) collective-permute-start(bf16[4,16,8,512]{3,2,1,0:T(8,128)(2,1)S(1)} %pad_maximum_fusion.refs_0_), channel_id=1, source_target_pairs={{0,16},{16,0},{1,17},{17,1},{2,18},{18,2},{3,19},{19,3},{4,20},{20... | collective-permute-start | bytes 1572872 | tf_op jit(solution)/shard_map/ppermute | solution.py:178
  98.1 8.3 %collective-permute-start.10 = (bf16[4,16,8,512]{3,2,1,0:T(8,128)(2,1)S(1)}, bf16[4,16,8,512]{3,2,1,0:T(8,128)(2,1)S(1)}, u32[]{:S(2)}, u32[]{:S(2)}) collective-permute-start(bf16[4,16,8,512]{3,2,1,0:T(8,128)(2,1)S(1)} %collective-permute-done.5.refs_2_), channel_id=1, source_target_pairs={{0,16},{16,0},{1,17},{17,1},{2,18},{18,2},{3,19},{19,3},{4,20},{20... | collective-permute-start | bytes 1572872 | tf_op jit(solution)/shard_map/ppermute | solution.py:178
  100.1 6.4 %collective-permute-start.9 = (bf16[4,16,8,512]{3,2,1,0:T(8,128)(2,1)S(1)}, bf16[4,16,8,512]{3,2,1,0:T(8,128)(2,1)}, u32[]{:S(2)}, u32[]{:S(2)}) collective-permute-start(bf16[4,16,8,512]{3,2,1,0:T(8,128)(2,1)S(1)} %collective-permute-done.4.refs_1_), channel_id=1, source_target_pairs={{0,16},{16,0},{1,17},{17,1},{2,18},{18,2},{3,19},{19,3},{4,20},{20... | collective-permute-start | bytes 1572872 | tf_op jit(solution)/shard_map/ppermute | solution.py:178
  102.5 4.8 %collective-permute-start.11 = (bf16[4,16,8,512]{3,2,1,0:T(8,128)(2,1)S(1)}, bf16[4,16,8,512]{3,2,1,0:T(8,128)(2,1)}, u32[]{:S(2)}, u32[]{:S(2)}) collective-permute-start(bf16[4,16,8,512]{3,2,1,0:T(8,128)(2,1)S(1)} %constant_dynamic-update-slice_fusion.refs_3_), channel_id=1, source_target_pairs={{0,16},{16,0},{1,17},{17,1},{2,18},{18,2},{3,19},{19,3},{4,20},{20... | collective-permute-start | bytes 1572872 | tf_op jit(solution)/shard_map/ppermute | solution.py:178
Sparse Core Ops, SparseCore 0:
  28.6 45.8 all-gather.3

commit v2 on v1

v2 whole, which is shorter than its diff:
```python
import math

import jax
import jax.numpy as jnp
import numpy as np
from jax import lax
from jax.experimental import pallas as pl
from jax.experimental.pallas import tpu as pltpu
from jax.sharding import Mesh, PartitionSpec as P

WINDOWS = 256
SAMPLES = 512
BINS = 16
LOW_BIN = 24
SPAN = 65
AXES = ("z", "yh", "core", "x", "yl")
SIZES = {"z": 8, "yh": 2, "core": 2, "x": 4, "yl": 4}
CHUNKS = 4
CHUNK = WINDOWS // CHUNKS
HALF = WINDOWS // 2


def dft_table():
    steps = np.arange(SAMPLES)
    freqs = LOW_BIN + np.arange(BINS)
    angles = (steps[None, :] * freqs[:, None] % SAMPLES) * (2.0 * math.pi / SAMPLES)
    dft = np.concatenate([np.cos(angles), -np.sin(angles)], axis=0).astype(np.float32)
    high = dft.astype(jnp.bfloat16)
    low = (dft - high.astype(np.float32)).astype(jnp.bfloat16)
    return np.concatenate([high, low], axis=0)


def nt_dot(left, right):
    return lax.dot_general(
        left, right, (((1,), (1,)), ((), ())), preferred_element_type=jnp.float32
    )


def whiten_kernel(raw_ref, dft_ref, out_ref, chunk_ref, table_ref, balanced_ref, white_ref, sems):
    rows = CHUNK * 8
    copies = [
        pltpu.make_async_copy(
            raw_ref.at[pl.ds(chunk * rows, rows)], chunk_ref.at[chunk], sems.at[chunk]
        )
        for chunk in range(CHUNKS)
    ]
    for copy in copies:
        copy.start()
    table_copy = pltpu.make_async_copy(dft_ref, table_ref, sems.at[CHUNKS])
    table_copy.start()
    here = lax.broadcasted_iota(jnp.int32, (SAMPLES, SAMPLES), 0)
    there = lax.broadcasted_iota(jnp.int32, (SAMPLES, SAMPLES), 1)
    near = jnp.abs(here - there) <= SPAN // 2
    band = jnp.where(near, 1.0, 0.0).astype(jnp.bfloat16)
    table_copy.wait()
    dft = table_ref[...]
    per_half = CHUNKS // 2
    for half in range(2):
        for part in range(per_half):
            chunk = half * per_half + part
            copies[chunk].wait()
            flat = chunk_ref[chunk]
            total = jnp.dot(jnp.abs(flat), band, preferred_element_type=jnp.float32)
            balanced = flat.astype(jnp.float32) / (total * (1.0 / SPAN) + 1e-06)
            for lane in range(4):
                balanced_ref[lane, pl.ds(chunk * rows, rows), :] = balanced[
                    :, lane * 128 : (lane + 1) * 128
                ]
        first = half * HALF * 8
        for channel in range(8):
            balanced = jnp.concatenate(
                [
                    balanced_ref[lane, pl.ds(first + channel, HALF, stride=8), :]
                    for lane in range(4)
                ],
                axis=1,
            )
            high = balanced.astype(jnp.bfloat16)
            low = (balanced - high.astype(jnp.float32)).astype(jnp.bfloat16)
            wide = nt_dot(dft, high)
            spectrum = wide[: 2 * BINS] + (wide[2 * BINS :] + nt_dot(dft[: 2 * BINS], low))
            real = spectrum[:BINS]
            imag = spectrum[BINS:]
            energy = real * real + imag * imag
            level = jnp.mean(energy, axis=0, keepdims=True)
            factor = lax.rsqrt(energy + 0.25 * level + 1.0)
            at = half * HALF
            white_ref[:, channel, at : at + HALF] = real * factor
            white_ref[:, channel, WINDOWS + at : WINDOWS + at + HALF] = imag * factor
    out_ref[...] = white_ref[...].astype(jnp.bfloat16)


def whiten(raw):
    anywhere = pl.BlockSpec(memory_space=pl.ANY)
    return pl.pallas_call(
        whiten_kernel,
        in_specs=[anywhere, anywhere],
        out_specs=pl.BlockSpec(memory_space=pltpu.VMEM),
        out_shape=jax.ShapeDtypeStruct((BINS, 8, 2 * WINDOWS), jnp.bfloat16),
        scratch_shapes=[
            pltpu.VMEM((CHUNKS, CHUNK * 8, SAMPLES), jnp.bfloat16),
            pltpu.VMEM((4 * BINS, SAMPLES), jnp.bfloat16),
            pltpu.VMEM((4, WINDOWS * 8, 128), jnp.float32),
            pltpu.VMEM((BINS, 8, 2 * WINDOWS), jnp.float32),
            pltpu.SemaphoreType.DMA((CHUNKS + 1,)),
        ],
        compiler_params=pltpu.CompilerParams(vmem_limit_bytes=60 << 20),
        cost_estimate=pl.CostEstimate(
            flops=3_000_000_000, bytes_accessed=3 << 20, transcendentals=1 << 20
        ),
        name="whiten",
    )(raw.reshape(WINDOWS * 8, SAMPLES), jnp.asarray(dft_table()))


def cross_kernel(place_ref, rows_ref, *refs):
    pieces = refs[:8]
    out_ref, left_ref, right_ref, tile_ref, row_sem, out_sem = refs[8:]
    row_copies = [
        pltpu.make_async_copy(rows_ref.at[k], left_ref.at[place_ref[32 + k]], row_sem.at[k])
        for k in range(16)
    ]
    for copy in row_copies:
        copy.start()

    def gather(b):
        k = 0
        for piece in pieces:
            for slot in range(piece.shape[0]):
                right_ref[b, place_ref[k]] = piece[slot, b]
                k += 1

    gather(0)
    for copy in row_copies:
        copy.wait()
    outs = []
    for b in range(BINS):
        if b + 1 < BINS:
            gather(b + 1)
        left = left_ref[:, b].reshape(128, 2 * WINDOWS)
        right = right_ref[b].reshape(256, 2 * WINDOWS)
        turned = jnp.concatenate([left[:, WINDOWS:], -left[:, :WINDOWS]], axis=1)
        both = jnp.concatenate([left, turned], axis=0)
        tile = (nt_dot(both, right) * (1.0 / WINDOWS)).astype(jnp.bfloat16)
        tile_ref[0, b] = tile[:128]
        tile_ref[1, b] = tile[128:]
        if b % 4 == 3:
            part = pl.ds(b - 3, 4)
            copy = pltpu.make_async_copy(
                tile_ref.at[:, part], out_ref.at[:, part], out_sem.at[b // 4]
            )
            copy.start()
            outs.append(copy)
    for copy in outs:
        copy.wait()


def cross(places, rows, pieces):
    block = (BINS, 8, 2 * WINDOWS)
    out = (2, BINS, 128, 256)
    anywhere = pl.BlockSpec(memory_space=pl.ANY)
    return pl.pallas_call(
        cross_kernel,
        in_specs=[pl.BlockSpec(memory_space=pltpu.SMEM), pl.BlockSpec(memory_space=pltpu.HBM)]
        + [pl.BlockSpec(memory_space=pltpu.VMEM)] * 8,
        out_specs=anywhere,
        out_shape=jax.ShapeDtypeStruct(out, jnp.bfloat16),
        scratch_shapes=[
            pltpu.VMEM((16,) + block, jnp.bfloat16),
            pltpu.VMEM((BINS, 32, 8, 2 * WINDOWS), jnp.bfloat16),
            pltpu.VMEM(out, jnp.bfloat16),
            pltpu.SemaphoreType.DMA((16,)),
            pltpu.SemaphoreType.DMA((4,)),
        ],
        compiler_params=pltpu.CompilerParams(vmem_limit_bytes=40 << 20),
        cost_estimate=pl.CostEstimate(
            flops=1_100_000_000, bytes_accessed=8 << 20, transcendentals=0
        ),
        name="cross",
    )(places, rows, *pieces)


def flat(z, yh, core, x, yl):
    return (((z * 2 + yh) * 2 + core) * 4 + x) * 4 + yl


def everyone():
    for index in np.ndindex(*(SIZES[a] for a in AXES)):
        yield index


def spread_pairs(turn):
    pairs = []
    for z, yh, core, x, yl in everyone():
        home = z * 2 + yh
        target = (turn + x) % 4
        layer = (x + yl + z) % 4 + 4 * (target // 2)
        pairs.append((flat(z, yh, core, x, yl), flat(layer, target % 2, core, home // 4, home % 4)))
    return pairs


def ring(value, axis, by):
    n = SIZES[axis]
    return lax.ppermute(value, axis, [(i, (i + by) % n) for i in range(n)])


def swap(value):
    return ring(value, "core", 1)


def places_here():
    table = []
    for z, yh, core, x, yl in everyone():
        home_z = (x * 4 + yl) // 2
        row = []
        for side in (core, 1 - core):
            for away, slots in ((0, 4), (-1, 4), (1, 4), (-2, 2), (2, 2)):
                layer = (z + away) % 8
                for slot in range(slots):
                    from_x = (2 * (layer // 4) + yh - slot) % 4
                    row.append(side * 16 + from_x * 4 + (layer - from_x - home_z) % 4)
        assert sorted(row) == list(range(32))
        row.extend(k // 4 * 4 + (yl - k % 4) % 4 for k in range(16))
        table.append(row)
    table = jnp.asarray(np.array(table, np.int32))
    return lax.dynamic_index_in_dim(table, lax.axis_index(AXES), keepdims=False)


def on_device(raw):
    white = whiten(raw)
    here = jnp.stack([lax.ppermute(white, AXES, spread_pairs(turn)) for turn in range(4)])
    near = jnp.stack([white] + [ring(white, "yl", by) for by in (1, 2, 3)])
    rows = lax.all_gather(near, "x").reshape((16,) + white.shape)
    below = ring(here, "z", 1)
    above = ring(here, "z", -1)
    far = jnp.concatenate([ring(below[:2], "z", 1), ring(above[:2], "z", -1)])
    mine = [here, below, above, far]
    pieces = mine + [swap(piece) for piece in mine]
    return cross(places_here(), rows, pieces)


def solution(mesh):
    split = Mesh(mesh.devices.reshape([SIZES[a] for a in AXES]), AXES)
    return jax.shard_map(
        on_device,
        mesh=split,
        in_specs=(P(None, AXES, None),),
        out_specs=P(None, None, ("z", "yh", "core"), ("x", "yl")),
        check_vma=False,
    )
```

time: 124 us -> 129 us (1.040)
  blocking collectives: 14.8 us -> 0 us
  waiting for transfers between devices: 25.8 us -> 37 us
  starting transfers between devices: 52 us -> 61.3 us
  local copies, waits for them, and re-layouts: 4.24 us -> 2.37 us
  other arithmetic: 0.07 us -> 1.83 us
    all_gather x1 -> x0, blocking collectives: 14.8 us -> none  [on_device(): rows = lax.all_gather(lax.all_gather(white, 'yl'), 'x')]
    ppermute x8 -> x11, starting transfers between devices: 32 us -> 42.2 us  [ring(): return lax.ppermute(value, axis, [(i, (i + by) % n) for i in range(n)])]
    ppermute x8 -> x11, waiting for transfers between devices: 8.38 us -> 18.2 us  [ring(): return lax.ppermute(value, axis, [(i, (i + by) % n) for i in range(n)])]
    pallas_call x1, Pallas kernels: 9.66 us -> 6.45 us  [cross(): pl.pallas_call(cross_kernel, in_specs=[pl.BlockSpec(memory_space=pltpu.SM...]
    pallas_call x1, Pallas kernels: 3.68 us -> 6.1 us  [whiten(): pl.pallas_call(whiten_kernel, in_specs=[anywhere, anywhere], out_specs=pl...]
    unnamed x7 -> x3, local copies, waits for them, and re-layouts: 3.49 us -> 1.61 us
    another operation x0 -> x1, other arithmetic: none -> 1.76 us  [on_device(): near = jnp.stack([white] + [ring(white, 'yl', by) for by in (1, 2, 3)])]
    ppermute x4, waiting for transfers between devices: 17.4 us -> 18.8 us  [on_device(): lax.ppermute(white, AXES, spread_pairs(turn))]
  transfers between devices with their start and end apart: 13 -> 16, of which waited for: 4 -> 5; matrix products, arithmetic and copies ran while one was open for 1% -> 1% of each run, Pallas kernels for 0% -> 0%
where the time goes in v2:
time: 129 us
  starting transfers between devices  61.3 us (48%)
  waiting for transfers between devices  37 us (29%)
  between operations  13.6 us (11%)
  Pallas kernels  12.6 us (10%)
  local copies, waits for them, and re-layouts  2.37 us (2%)
  other arithmetic  1.83 us (1%)
    ppermute x11, starting transfers between devices, ring(): return lax.ppermute(value, axis, [(i, (i + by) % n) for i in range(n)])  42.2 us
    ppermute x4, starting transfers between devices, on_device(): lax.ppermute(white, AXES, spread_pairs(turn))  19.1 us
    ppermute x4, waiting for transfers between devices, on_device(): lax.ppermute(white, AXES, spread_pairs(turn))  18.8 us
    ppermute x11, waiting for transfers between devices, ring(): return lax.ppermute(value, axis, [(i, (i + by) % n) for i in range(n)])  18.2 us
    pallas_call x1, Pallas kernels, cross(): pl.pallas_call(cross_kernel, in_specs=[pl.BlockSpec(memory_space=pltpu.SM...  6.45 us
    pallas_call x1, Pallas kernels, whiten(): pl.pallas_call(whiten_kernel, in_specs=[anywhere, anywhere], out_specs=pl...  6.1 us
  transfers between devices with their start and end apart: 16, of which 5 were waited for; matrix products, arithmetic and copies ran while one was open for 1% of the time, Pallas kernels for 0%

profile of v2, /device:TPU:193, one launch (start us, length us, event | category | flops | bytes accessed | tf_op | source)
XLA Modules:
  0.0 128.6 jit_solution(9338496093651656006)
XLA Ops:
  6.5 6.1 %whiten.1 = bf16[16,8,512]{2,1,0:T(8,128)(2,1)} custom-call(bf16[2048,512]{1,0:T(8,128)(2,1)} %bitcast.19, bf16[64,512]{1,0:T(8,128)(2,1)} %constant.41.clone.dft_ref), custom_call_target="tpu_custom_call" | custom-call | flops 3000000000 | bytes 3145728 | tf_op jit(solution)/shard_map/whiten/pallas_call | solution.py:95
  12.6 5.2 %collective-permute-start.2 = (bf16[16,8,512]{2,1,0:T(8,128)(2,1)}, bf16[16,8,512]{2,1,0:T(8,128)(2,1)S(1)}, u32[]{:S(2)}, u32[]{:S(2)}) collective-permute-start(bf16[16,8,512]{2,1,0:T(8,128)(2,1)} %whiten.1), channel_id=1, source_target_pairs={{0,3},{1,0},{2,1},{3,2},{4,7},{5,4},{6,5},{7,6},{8,11},{9,8},{10,9... | collective-permute-start | bytes 393224 | tf_op jit(solution)/shard_map/ppermute | solution.py:203
  17.9 1.9 %collective-permute-start.1 = (bf16[16,8,512]{2,1,0:T(8,128)(2,1)}, bf16[16,8,512]{2,1,0:T(8,128)(2,1)S(1)}, u32[]{:S(2)}, u32[]{:S(2)}) collective-permute-start(bf16[16,8,512]{2,1,0:T(8,128)(2,1)} %whiten.1), channel_id=1, source_target_pairs={{0,2},{1,3},{2,0},{3,1},{4,6},{5,7},{6,4},{7,5},{8,10},{9,11},{10,... | collective-permute-start | bytes 393224 | tf_op jit(solution)/shard_map/ppermute | solution.py:203
  19.8 2.3 %collective-permute-start = (bf16[16,8,512]{2,1,0:T(8,128)(2,1)}, bf16[16,8,512]{2,1,0:T(8,128)(2,1)S(1)}, u32[]{:S(2)}, u32[]{:S(2)}) collective-permute-start(bf16[16,8,512]{2,1,0:T(8,128)(2,1)} %whiten.1), channel_id=1, source_target_pairs={{0,1},{1,2},{2,3},{3,0},{4,5},{5,6},{6,7},{7,4},{8,9},{9,10},{10,1... | collective-permute-start | bytes 393224 | tf_op jit(solution)/shard_map/ppermute | solution.py:203
  22.2 8.4 %collective-permute-done.1 = bf16[16,8,512]{2,1,0:T(8,128)(2,1)S(1)} collective-permute-done((bf16[16,8,512]{2,1,0:T(8,128)(2,1)}, bf16[16,8,512]{2,1,0:T(8,128)(2,1)S(1)}, u32[]{:S(2)}, u32[]{:S(2)}) %collective-permute-start.1) | collective-permute-done | bytes 131104 | tf_op jit(solution)/shard_map/ppermute | solution.py:203
  30.6 1.8 %pad_maximum_fusion = bf16[4,16,8,512]{3,2,1,0:T(8,128)(2,1)} fusion(bf16[1,16,8,512]{3,2,1,0:T(8,128)(2,1)S(1)} %bitcast.15, bf16[1,16,8,512]{3,2,1,0:T(8,128)(2,1)S(1)} %bitcast.17, bf16[1,16,8,512]{3,2,1,0:T(8,128)(2,1)S(1)} %bitcast.18, bf16[1,16,8,512]{3,2,1,0:T(8,128)(2,1)} %bitcast.11), kind=kLoop, calls=%fused_computation | loop fusion | flops 786432 | bytes 1048576 | tf_op jit(solution)/shard_map/stack | solution.py:231
  32.4 11.6 %collective-permute-start.6 = (bf16[16,8,512]{2,1,0:T(8,128)(2,1)}, bf16[16,8,512]{2,1,0:T(8,128)(2,1)S(1)}, u32[]{:S(2)}, u32[]{:S(2)}) collective-permute-start(bf16[16,8,512]{2,1,0:T(8,128)(2,1)} %whiten.1), channel_id=1, source_target_pairs={{0,288},{1,352},{2,416},{3,480},{4,64},{5,128},{6,192},{7,0},{8,16... | collective-permute-start | bytes 393224 | tf_op jit(solution)/shard_map/ppermute | solution.py:230
  44.0 1.9 %collective-permute-start.5 = (bf16[16,8,512]{2,1,0:T(8,128)(2,1)}, bf16[16,8,512]{2,1,0:T(8,128)(2,1)S(1)}, u32[]{:S(2)}, u32[]{:S(2)}) collective-permute-start(bf16[16,8,512]{2,1,0:T(8,128)(2,1)} %whiten.1), channel_id=1, source_target_pairs={{0,256},{1,320},{2,384},{3,448},{4,352},{5,416},{6,480},{7,288},{8... | collective-permute-start | bytes 393224 | tf_op jit(solution)/shard_map/ppermute | solution.py:230
  45.9 1.9 %collective-permute-start.4 = (bf16[16,8,512]{2,1,0:T(8,128)(2,1)}, bf16[16,8,512]{2,1,0:T(8,128)(2,1)S(1)}, u32[]{:S(2)}, u32[]{:S(2)}) collective-permute-start(bf16[16,8,512]{2,1,0:T(8,128)(2,1)} %whiten.1), channel_id=1, source_target_pairs={{0,32},{1,96},{2,160},{3,224},{4,320},{5,384},{6,448},{7,256},{8,4... | collective-permute-start | bytes 393224 | tf_op jit(solution)/shard_map/ppermute | solution.py:230
  47.9 3.6 %collective-permute-start.3 = (bf16[16,8,512]{2,1,0:T(8,128)(2,1)}, bf16[16,8,512]{2,1,0:T(8,128)(2,1)S(1)}, u32[]{:S(2)}, u32[]{:S(2)}) collective-permute-start(bf16[16,8,512]{2,1,0:T(8,128)(2,1)} %whiten.1), channel_id=1, source_target_pairs={{0,0},{1,64},{2,128},{3,192},{4,96},{5,160},{6,224},{7,32},{8,384}... | collective-permute-start | bytes 393224 | tf_op jit(solution)/shard_map/ppermute | solution.py:230
  51.5 13.5 %collective-permute-done.5 = bf16[16,8,512]{2,1,0:T(8,128)(2,1)S(1)} collective-permute-done((bf16[16,8,512]{2,1,0:T(8,128)(2,1)}, bf16[16,8,512]{2,1,0:T(8,128)(2,1)S(1)}, u32[]{:S(2)}, u32[]{:S(2)}) %collective-permute-start.5) | collective-permute-done | bytes 131104 | tf_op jit(solution)/shard_map/ppermute | solution.py:230
  65.0 5.3 %collective-permute-done.3 = bf16[16,8,512]{2,1,0:T(8,128)(2,1)S(1)} collective-permute-done((bf16[16,8,512]{2,1,0:T(8,128)(2,1)}, bf16[16,8,512]{2,1,0:T(8,128)(2,1)S(1)}, u32[]{:S(2)}, u32[]{:S(2)}) %collective-permute-start.3) | collective-permute-done | bytes 131104 | tf_op jit(solution)/shard_map/ppermute | solution.py:230
  70.4 11.8 %collective-permute-start.7 = (bf16[4,16,8,512]{3,2,1,0:T(8,128)(2,1)S(1)}, bf16[4,16,8,512]{3,2,1,0:T(8,128)(2,1)S(1)}, u32[]{:S(2)}, u32[]{:S(2)}) collective-permute-start(bf16[4,16,8,512]{3,2,1,0:T(8,128)(2,1)S(1)} %pad_maximum_fusion.1.refs_0_), channel_id=1, source_target_pairs={{0,64},{64,128},{128,192},{192,256},{256,320},{320,384},{384,448},... | collective-permute-start | bytes 1572872 | tf_op jit(solution)/shard_map/ppermute | solution.py:203
  82.2 1.9 %collective-permute-start.8 = (bf16[4,16,8,512]{3,2,1,0:T(8,128)(2,1)S(1)}, bf16[4,16,8,512]{3,2,1,0:T(8,128)(2,1)S(1)}, u32[]{:S(2)}, u32[]{:S(2)}) collective-permute-start(bf16[4,16,8,512]{3,2,1,0:T(8,128)(2,1)S(1)} %pad_maximum_fusion.1.refs_0_), channel_id=1, source_target_pairs={{0,448},{64,0},{128,64},{192,128},{256,192},{320,256},{384,320},{4... | collective-permute-start | bytes 1572872 | tf_op jit(solution)/shard_map/ppermute | solution.py:203
  84.1 8.8 %collective-permute-done.7.refs_1_ = bf16[4,16,8,512]{3,2,1,0:T(8,128)(2,1)S(1)} collective-permute-done((bf16[4,16,8,512]{3,2,1,0:T(8,128)(2,1)S(1)}, bf16[4,16,8,512]{3,2,1,0:T(8,128)(2,1)S(1)}, u32[]{:S(2)}, u32[]{:S(2)}) %collective-permute-start.7) | collective-permute-done | bytes 524320 | tf_op jit(solution)/shard_map/ppermute | solution.py:203
  92.9 5.3 %collective-permute-start.9 = (bf16[2,16,8,512]{3,2,1,0:T(8,128)(2,1)S(1)}, bf16[2,16,8,512]{3,2,1,0:T(8,128)(2,1)S(1)}, u32[]{:S(2)}, u32[]{:S(2)}) collective-permute-start(bf16[2,16,8,512]{3,2,1,0:T(8,128)(2,1)S(1)} %slice.8), channel_id=1, source_target_pairs={{0,64},{64,128},{128,192},{192,256},{256,320},{320,384},{384,448},... | collective-permute-start | bytes 786440 | tf_op jit(solution)/shard_map/ppermute | solution.py:203
  98.3 1.9 %collective-permute-start.10 = (bf16[2,16,8,512]{3,2,1,0:T(8,128)(2,1)S(1)}, bf16[2,16,8,512]{3,2,1,0:T(8,128)(2,1)S(1)}, u32[]{:S(2)}, u32[]{:S(2)}) collective-permute-start(bf16[2,16,8,512]{3,2,1,0:T(8,128)(2,1)S(1)} %slice.9), channel_id=1, source_target_pairs={{0,448},{64,0},{128,64},{192,128},{256,192},{320,256},{384,320},{4... | collective-permute-start | bytes 786440 | tf_op jit(solution)/shard_map/ppermute | solution.py:203
  100.2 3.6 %collective-permute-start.11 = (bf16[4,16,8,512]{3,2,1,0:T(8,128)(2,1)S(1)}, bf16[4,16,8,512]{3,2,1,0:T(8,128)(2,1)S(1)}, u32[]{:S(2)}, u32[]{:S(2)}) collective-permute-start(bf16[4,16,8,512]{3,2,1,0:T(8,128)(2,1)S(1)} %pad_maximum_fusion.1.refs_0_), channel_id=1, source_target_pairs={{0,16},{16,0},{1,17},{17,1},{2,18},{18,2},{3,19},{19,3},{4,20},{20... | collective-permute-start | bytes 1572872 | tf_op jit(solution)/shard_map/ppermute | solution.py:203
  103.8 1.9 %collective-permute-start.13 = (bf16[4,16,8,512]{3,2,1,0:T(8,128)(2,1)S(1)}, bf16[4,16,8,512]{3,2,1,0:T(8,128)(2,1)S(1)}, u32[]{:S(2)}, u32[]{:S(2)}) collective-permute-start(bf16[4,16,8,512]{3,2,1,0:T(8,128)(2,1)S(1)} %collective-permute-done.8.refs_2_), channel_id=1, source_target_pairs={{0,16},{16,0},{1,17},{17,1},{2,18},{18,2},{3,19},{19,3},{4,20},{20... | collective-permute-start | bytes 1572872 | tf_op jit(solution)/shard_map/ppermute | solution.py:203
  105.8 2.4 %collective-permute-start.12 = (bf16[4,16,8,512]{3,2,1,0:T(8,128)(2,1)S(1)}, bf16[4,16,8,512]{3,2,1,0:T(8,128)(2,1)}, u32[]{:S(2)}, u32[]{:S(2)}) collective-permute-start(bf16[4,16,8,512]{3,2,1,0:T(8,128)(2,1)S(1)} %collective-permute-done.7.refs_1_), channel_id=1, source_target_pairs={{0,16},{16,0},{1,17},{17,1},{2,18},{18,2},{3,19},{19,3},{4,20},{20... | collective-permute-start | bytes 1572872 | tf_op jit(solution)/shard_map/ppermute | solution.py:203
  108.3 3.8 %collective-permute-start.14 = (bf16[4,16,8,512]{3,2,1,0:T(8,128)(2,1)S(1)}, bf16[4,16,8,512]{3,2,1,0:T(8,128)(2,1)}, u32[]{:S(2)}, u32[]{:S(2)}) collective-permute-start(bf16[4,16,8,512]{3,2,1,0:T(8,128)(2,1)S(1)} %constant_dynamic-update-slice_fusion.refs_3_), channel_id=1, source_target_pairs={{0,16},{16,0},{1,17},{17,1},{2,18},{18,2},{3,19},{19,3},{4,20},{20... | collective-permute-start | bytes 1572872 | tf_op jit(solution)/shard_map/ppermute | solution.py:203
  112.8 0.9 collective-permute-done.14.refs_7_
  113.7 1.6 %copy-done = bf16[16,16,8,512]{3,2,1,0:T(8,128)(2,1)S(1)} copy-done((bf16[16,16,8,512]{3,2,1,0:T(8,128)(2,1)S(1)}, bf16[16,16,8,512]{3,2,1,0:T(8,128)(2,1)}, u32[]{:S(2)}) %copy-start) | copy-done | bytes 2097176
  115.3 6.4 %cross.1 = bf16[2,16,128,256]{3,2,1,0:T(8,128)(2,1)} custom-call(s32[48]{0:T(128)S(1)} %dynamic-slice_bitcast_fusion.place_ref, bf16[16,16,8,512]{3,2,1,0:T(8,128)(2,1)S(1)} %copy-done, bf16[4,16,8,512]{3,2,1,0:T(8,128)(2,1)S(1)} %pad_maximum_fusion.1.refs_0_, bf16[4,16,8,512]{3,2,1,0:T(8,128)(2,1)S(1)} %collective-permute-done.7.refs_1_, ...), custom_call_target="tpu_custom_call" | custom-call | flops 1100000000 | bytes 8388608 | tf_op jit(solution)/shard_map/cross/pallas_call | solution.py:161
  (20 shorter events, 0.9 us)
Async XLA Ops:
  6.5 107.2 %all-gather.3.cloned.1.call-start = ((), (), s32[]{:S(2)}) async-start(), calls=%async_computation | async-start | bytes 2621440 | tf_op jit(solution)/shard_map/all_gather | solution.py:232
  12.6 9.5 %collective-permute-start.2 = (bf16[16,8,512]{2,1,0:T(8,128)(2,1)}, bf16[16,8,512]{2,1,0:T(8,128)(2,1)S(1)}, u32[]{:S(2)}, u32[]{:S(2)}) collective-permute-start(bf16[16,8,512]{2,1,0:T(8,128)(2,1)} %whiten.1), channel_id=1, source_target_pairs={{0,3},{1,0},{2,1},{3,2},{4,7},{5,4},{6,5},{7,6},{8,11},{9,8},{10,9... | collective-permute-start | bytes 393224 | tf_op jit(solution)/shard_map/ppermute | solution.py:203
  17.9 12.7 %collective-permute-start.1 = (bf16[16,8,512]{2,1,0:T(8,128)(2,1)}, bf16[16,8,512]{2,1,0:T(8,128)(2,1)S(1)}, u32[]{:S(2)}, u32[]{:S(2)}) collective-permute-start(bf16[16,8,512]{2,1,0:T(8,128)(2,1)} %whiten.1), channel_id=1, source_target_pairs={{0,2},{1,3},{2,0},{3,1},{4,6},{5,7},{6,4},{7,5},{8,10},{9,11},{10,... | collective-permute-start | bytes 393224 | tf_op jit(solution)/shard_map/ppermute | solution.py:203
  19.8 10.8 %collective-permute-start = (bf16[16,8,512]{2,1,0:T(8,128)(2,1)}, bf16[16,8,512]{2,1,0:T(8,128)(2,1)S(1)}, u32[]{:S(2)}, u32[]{:S(2)}) collective-permute-start(bf16[16,8,512]{2,1,0:T(8,128)(2,1)} %whiten.1), channel_id=1, source_target_pairs={{0,1},{1,2},{2,3},{3,0},{4,5},{5,6},{6,7},{7,4},{8,9},{9,10},{10,1... | collective-permute-start | bytes 393224 | tf_op jit(solution)/shard_map/ppermute | solution.py:203
  32.4 19.1 %collective-permute-start.6 = (bf16[16,8,512]{2,1,0:T(8,128)(2,1)}, bf16[16,8,512]{2,1,0:T(8,128)(2,1)S(1)}, u32[]{:S(2)}, u32[]{:S(2)}) collective-permute-start(bf16[16,8,512]{2,1,0:T(8,128)(2,1)} %whiten.1), channel_id=1, source_target_pairs={{0,288},{1,352},{2,416},{3,480},{4,64},{5,128},{6,192},{7,0},{8,16... | collective-permute-start | bytes 393224 | tf_op jit(solution)/shard_map/ppermute | solution.py:230
  44.0 21.0 %collective-permute-start.5 = (bf16[16,8,512]{2,1,0:T(8,128)(2,1)}, bf16[16,8,512]{2,1,0:T(8,128)(2,1)S(1)}, u32[]{:S(2)}, u32[]{:S(2)}) collective-permute-start(bf16[16,8,512]{2,1,0:T(8,128)(2,1)} %whiten.1), channel_id=1, source_target_pairs={{0,256},{1,320},{2,384},{3,448},{4,352},{5,416},{6,480},{7,288},{8... | collective-permute-start | bytes 393224 | tf_op jit(solution)/shard_map/ppermute | solution.py:230
  45.9 19.1 %collective-permute-start.4 = (bf16[16,8,512]{2,1,0:T(8,128)(2,1)}, bf16[16,8,512]{2,1,0:T(8,128)(2,1)S(1)}, u32[]{:S(2)}, u32[]{:S(2)}) collective-permute-start(bf16[16,8,512]{2,1,0:T(8,128)(2,1)} %whiten.1), channel_id=1, source_target_pairs={{0,32},{1,96},{2,160},{3,224},{4,320},{5,384},{6,448},{7,256},{8,4... | collective-permute-start | bytes 393224 | tf_op jit(solution)/shard_map/ppermute | solution.py:230
  47.9 22.4 %collective-permute-start.3 = (bf16[16,8,512]{2,1,0:T(8,128)(2,1)}, bf16[16,8,512]{2,1,0:T(8,128)(2,1)S(1)}, u32[]{:S(2)}, u32[]{:S(2)}) collective-permute-start(bf16[16,8,512]{2,1,0:T(8,128)(2,1)} %whiten.1), channel_id=1, source_target_pairs={{0,0},{1,64},{2,128},{3,192},{4,96},{5,160},{6,224},{7,32},{8,384}... | collective-permute-start | bytes 393224 | tf_op jit(solution)/shard_map/ppermute | solution.py:230
  70.4 22.5 %collective-permute-start.7 = (bf16[4,16,8,512]{3,2,1,0:T(8,128)(2,1)S(1)}, bf16[4,16,8,512]{3,2,1,0:T(8,128)(2,1)S(1)}, u32[]{:S(2)}, u32[]{:S(2)}) collective-permute-start(bf16[4,16,8,512]{3,2,1,0:T(8,128)(2,1)S(1)} %pad_maximum_fusion.1.refs_0_), channel_id=1, source_target_pairs={{0,64},{64,128},{128,192},{192,256},{256,320},{320,384},{384,448},... | collective-permute-start | bytes 1572872 | tf_op jit(solution)/shard_map/ppermute | solution.py:203
  82.2 16.1 %collective-permute-start.8 = (bf16[4,16,8,512]{3,2,1,0:T(8,128)(2,1)S(1)}, bf16[4,16,8,512]{3,2,1,0:T(8,128)(2,1)S(1)}, u32[]{:S(2)}, u32[]{:S(2)}) collective-permute-start(bf16[4,16,8,512]{3,2,1,0:T(8,128)(2,1)S(1)} %pad_maximum_fusion.1.refs_0_), channel_id=1, source_target_pairs={{0,448},{64,0},{128,64},{192,128},{256,192},{320,256},{384,320},{4... | collective-permute-start | bytes 1572872 | tf_op jit(solution)/shard_map/ppermute | solution.py:203
  92.9 15.2 %collective-permute-start.9 = (bf16[2,16,8,512]{3,2,1,0:T(8,128)(2,1)S(1)}, bf16[2,16,8,512]{3,2,1,0:T(8,128)(2,1)S(1)}, u32[]{:S(2)}, u32[]{:S(2)}) collective-permute-start(bf16[2,16,8,512]{3,2,1,0:T(8,128)(2,1)S(1)} %slice.8), channel_id=1, source_target_pairs={{0,64},{64,128},{128,192},{192,256},{256,320},{320,384},{384,448},... | collective-permute-start | bytes 786440 | tf_op jit(solution)/shard_map/ppermute | solution.py:203
  98.3 9.9 %collective-permute-start.10 = (bf16[2,16,8,512]{3,2,1,0:T(8,128)(2,1)S(1)}, bf16[2,16,8,512]{3,2,1,0:T(8,128)(2,1)S(1)}, u32[]{:S(2)}, u32[]{:S(2)}) collective-permute-start(bf16[2,16,8,512]{3,2,1,0:T(8,128)(2,1)S(1)} %slice.9), channel_id=1, source_target_pairs={{0,448},{64,0},{128,64},{192,128},{256,192},{320,256},{384,320},{4... | collective-permute-start | bytes 786440 | tf_op jit(solution)/shard_map/ppermute | solution.py:203
  100.2 12.6 %collective-permute-start.11 = (bf16[4,16,8,512]{3,2,1,0:T(8,128)(2,1)S(1)}, bf16[4,16,8,512]{3,2,1,0:T(8,128)(2,1)S(1)}, u32[]{:S(2)}, u32[]{:S(2)}) collective-permute-start(bf16[4,16,8,512]{3,2,1,0:T(8,128)(2,1)S(1)} %pad_maximum_fusion.1.refs_0_), channel_id=1, source_target_pairs={{0,16},{16,0},{1,17},{17,1},{2,18},{18,2},{3,19},{19,3},{4,20},{20... | collective-permute-start | bytes 1572872 | tf_op jit(solution)/shard_map/ppermute | solution.py:203
  103.8 8.9 %collective-permute-start.13 = (bf16[4,16,8,512]{3,2,1,0:T(8,128)(2,1)S(1)}, bf16[4,16,8,512]{3,2,1,0:T(8,128)(2,1)S(1)}, u32[]{:S(2)}, u32[]{:S(2)}) collective-permute-start(bf16[4,16,8,512]{3,2,1,0:T(8,128)(2,1)S(1)} %collective-permute-done.8.refs_2_), channel_id=1, source_target_pairs={{0,16},{16,0},{1,17},{17,1},{2,18},{18,2},{3,19},{19,3},{4,20},{20... | collective-permute-start | bytes 1572872 | tf_op jit(solution)/shard_map/ppermute | solution.py:203
  105.8 7.0 %collective-permute-start.12 = (bf16[4,16,8,512]{3,2,1,0:T(8,128)(2,1)S(1)}, bf16[4,16,8,512]{3,2,1,0:T(8,128)(2,1)}, u32[]{:S(2)}, u32[]{:S(2)}) collective-permute-start(bf16[4,16,8,512]{3,2,1,0:T(8,128)(2,1)S(1)} %collective-permute-done.7.refs_1_), channel_id=1, source_target_pairs={{0,16},{16,0},{1,17},{17,1},{2,18},{18,2},{3,19},{19,3},{4,20},{20... | collective-permute-start | bytes 1572872 | tf_op jit(solution)/shard_map/ppermute | solution.py:203
  108.3 5.5 %collective-permute-start.14 = (bf16[4,16,8,512]{3,2,1,0:T(8,128)(2,1)S(1)}, bf16[4,16,8,512]{3,2,1,0:T(8,128)(2,1)}, u32[]{:S(2)}, u32[]{:S(2)}) collective-permute-start(bf16[4,16,8,512]{3,2,1,0:T(8,128)(2,1)S(1)} %constant_dynamic-update-slice_fusion.refs_3_), channel_id=1, source_target_pairs={{0,16},{16,0},{1,17},{17,1},{2,18},{18,2},{3,19},{19,3},{4,20},{20... | collective-permute-start | bytes 1572872 | tf_op jit(solution)/shard_map/ppermute | solution.py:203
  113.7 1.6 %copy-start = (bf16[16,16,8,512]{3,2,1,0:T(8,128)(2,1)S(1)}, bf16[16,16,8,512]{3,2,1,0:T(8,128)(2,1)}, u32[]{:S(2)}) copy-start(bf16[16,16,8,512]{3,2,1,0:T(8,128)(2,1)} %all-gather.3.cloned.1.call-done.rows_ref) | copy-start | bytes 6291460
Sparse Core Ops, SparseCore 0:
  32.5 42.6 all-gather.2

commit v3 on v2

--- a/solution.py
+++ b/solution.py
@@ -1,3 +1,4 @@
+import itertools
 import math
 
 import jax
@@ -18,6 +19,7 @@
 CHUNKS = 4
 CHUNK = WINDOWS // CHUNKS
 HALF = WINDOWS // 2
+GROUP = 4
 
 
 def dft_table():
@@ -112,41 +114,35 @@
     )(raw.reshape(WINDOWS * 8, SAMPLES), jnp.asarray(dft_table()))
 
 
-def cross_kernel(place_ref, rows_ref, *refs):
-    pieces = refs[:8]
-    out_ref, left_ref, right_ref, tile_ref, row_sem, out_sem = refs[8:]
-    row_copies = [
-        pltpu.make_async_copy(rows_ref.at[k], left_ref.at[place_ref[32 + k]], row_sem.at[k])
-        for k in range(16)
-    ]
-    for copy in row_copies:
-        copy.start()
+def multiply(left, right):
+    turned = jnp.concatenate([left[:, WINDOWS:], -left[:, :WINDOWS]], axis=1)
+    both = jnp.concatenate([left, turned], axis=0)
+    tile = (nt_dot(both, right) * (1.0 / WINDOWS)).astype(jnp.bfloat16)
+    return tile[:128], tile[128:]
+
+
+def cross_kernel(place_ref, *refs):
+    count = len(refs) - 5
+    pieces = refs[:count]
+    out_ref, left_ref, right_ref, tile_ref, out_sem = refs[count:]
 
     def gather(b):
-        k = 0
-        for piece in pieces:
-            for slot in range(piece.shape[0]):
-                right_ref[b, place_ref[k]] = piece[slot, b]
-                k += 1
+        for k, piece in enumerate(pieces):
+            target = left_ref if k < 4 else right_ref
+            target[b, place_ref[k]] = piece[:, b]
 
     gather(0)
-    for copy in row_copies:
-        copy.wait()
     outs = []
     for b in range(BINS):
         if b + 1 < BINS:
             gather(b + 1)
-        left = left_ref[:, b].reshape(128, 2 * WINDOWS)
+        left = left_ref[b].reshape(128, 2 * WINDOWS)
         right = right_ref[b].reshape(256, 2 * WINDOWS)
-        turned = jnp.concatenate([left[:, WINDOWS:], -left[:, :WINDOWS]], axis=1)
-        both = jnp.concatenate([left, turned], axis=0)
-        tile = (nt_dot(both, right) * (1.0 / WINDOWS)).astype(jnp.bfloat16)
-        tile_ref[0, b] = tile[:128]
-        tile_ref[1, b] = tile[128:]
-        if b % 4 == 3:
-            part = pl.ds(b - 3, 4)
+        tile_ref[0, b], tile_ref[1, b] = multiply(left, right)
+        if b % GROUP == GROUP - 1:
+            bins = pl.ds(b - GROUP + 1, GROUP)
             copy = pltpu.make_async_copy(
-                tile_ref.at[:, part], out_ref.at[:, part], out_sem.at[b // 4]
+                tile_ref.at[:, bins], out_ref.at[:, bins], out_sem.at[b // GROUP]
             )
             copy.start()
             outs.append(copy)
@@ -154,29 +150,26 @@
         copy.wait()
 
 
-def cross(places, rows, pieces):
-    block = (BINS, 8, 2 * WINDOWS)
+def cross(places, pieces):
     out = (2, BINS, 128, 256)
-    anywhere = pl.BlockSpec(memory_space=pl.ANY)
     return pl.pallas_call(
         cross_kernel,
-        in_specs=[pl.BlockSpec(memory_space=pltpu.SMEM), pl.BlockSpec(memory_space=pltpu.HBM)]
-        + [pl.BlockSpec(memory_space=pltpu.VMEM)] * 8,
-        out_specs=anywhere,
+        in_specs=[pl.BlockSpec(memory_space=pltpu.SMEM)]
+        + [pl.BlockSpec(memory_space=pltpu.VMEM)] * len(pieces),
+        out_specs=pl.BlockSpec(memory_space=pl.ANY),
         out_shape=jax.ShapeDtypeStruct(out, jnp.bfloat16),
         scratch_shapes=[
-            pltpu.VMEM((16,) + block, jnp.bfloat16),
-            pltpu.VMEM((BINS, 32, 8, 2 * WINDOWS), jnp.bfloat16),
+            pltpu.VMEM((BINS, 4, 4, 8, 2 * WINDOWS), jnp.bfloat16),
+            pltpu.VMEM((BINS, 8, 4, 8, 2 * WINDOWS), jnp.bfloat16),
             pltpu.VMEM(out, jnp.bfloat16),
-            pltpu.SemaphoreType.DMA((16,)),
-            pltpu.SemaphoreType.DMA((4,)),
+            pltpu.SemaphoreType.DMA((BINS // GROUP,)),
         ],
         compiler_params=pltpu.CompilerParams(vmem_limit_bytes=40 << 20),
         cost_estimate=pl.CostEstimate(
             flops=1_100_000_000, bytes_accessed=8 << 20, transcendentals=0
         ),
         name="cross",
-    )(places, rows, *pieces)
+    )(places, *pieces)
 
 
 def flat(z, yh, core, x, yl):
@@ -188,13 +181,33 @@
         yield index
 
 
-def spread_pairs(turn):
+def layer_class(z, x):
+    return (x + z + z // 2) % 4
+
+
+def ring_distance(a, b):
+    return min((a - b) % 8, (b - a) % 8)
+
+
+def spread_pairs():
     pairs = []
-    for z, yh, core, x, yl in everyone():
+    for z, yh, x in np.ndindex(8, 2, 4):
         home = z * 2 + yh
-        target = (turn + x) % 4
-        layer = (x + yl + z) % 4 + 4 * (target // 2)
-        pairs.append((flat(z, yh, core, x, yl), flat(layer, target % 2, core, home // 4, home % 4)))
+        layer = layer_class(z, x)
+        wanted = [(layer + 4 * up, half) for up in range(2) for half in range(2)]
+
+        def way(order):
+            return sum(
+                ring_distance(4 * yh + yl, 4 * half + home % 4)
+                for yl, (_, half) in enumerate(order)
+            )
+
+        order = min(itertools.permutations(wanted), key=way)
+        for yl, (to_z, half) in enumerate(order):
+            for core in range(2):
+                pairs.append(
+                    (flat(z, yh, core, x, yl), flat(to_z, half, core, home // 4, home % 4))
+                )
     return pairs
 
 
@@ -210,32 +223,31 @@
 def places_here():
     table = []
     for z, yh, core, x, yl in everyone():
+        rows = [(x + away) % 4 for away in (0, -1, 1, 2)]
+        cols = []
         home_z = (x * 4 + yl) // 2
-        row = []
         for side in (core, 1 - core):
-            for away, slots in ((0, 4), (-1, 4), (1, 4), (-2, 2), (2, 2)):
+            for away in (0, -1, 1, 2):
                 layer = (z + away) % 8
-                for slot in range(slots):
-                    from_x = (2 * (layer // 4) + yh - slot) % 4
-                    row.append(side * 16 + from_x * 4 + (layer - from_x - home_z) % 4)
-        assert sorted(row) == list(range(32))
-        row.extend(k // 4 * 4 + (yl - k % 4) % 4 for k in range(16))
-        table.append(row)
+                (from_x,) = (k for k in range(4) if layer_class(home_z, k) == layer % 4)
+                cols.append(side * 4 + from_x)
+        assert sorted(rows) == list(range(4)) and sorted(cols) == list(range(8))
+        table.append(rows + cols)
     table = jnp.asarray(np.array(table, np.int32))
     return lax.dynamic_index_in_dim(table, lax.axis_index(AXES), keepdims=False)
 
 
 def on_device(raw):
     white = whiten(raw)
-    here = jnp.stack([lax.ppermute(white, AXES, spread_pairs(turn)) for turn in range(4)])
-    near = jnp.stack([white] + [ring(white, "yl", by) for by in (1, 2, 3)])
-    rows = lax.all_gather(near, "x").reshape((16,) + white.shape)
+    near = lax.all_gather(white, "yl")
+    here = lax.ppermute(near, AXES, spread_pairs())
+    rows = [near] + [ring(near, "x", by) for by in (1, -1, 2)]
     below = ring(here, "z", 1)
     above = ring(here, "z", -1)
-    far = jnp.concatenate([ring(below[:2], "z", 1), ring(above[:2], "z", -1)])
+    far = jnp.concatenate([ring(below[:2], "z", 1), ring(above[2:], "z", -1)])
     mine = [here, below, above, far]
-    pieces = mine + [swap(piece) for piece in mine]
-    return cross(places_here(), rows, pieces)
+    pieces = rows + mine + [swap(piece) for piece in mine]
+    return cross(places_here(), pieces)
 
 
 def solution(mesh):

time: 129 us -> 106 us (0.82)
  the two profiles are of different devices: /device:TPU:193 before, /device:TPU:19 now
where the time goes in v3:
time: 106 us
  starting transfers between devices  62.3 us (59%)
  waiting for transfers between devices  17.8 us (17%)
  blocking collectives  13 us (12%)
  Pallas kernels  10 us (9%)
  local copies, waits for them, and re-layouts  2.61 us (2%)
    ppermute x11, starting transfers between devices, ring(): return lax.ppermute(value, axis, [(i, (i + by) % n) for i in range(n)])  55.7 us
    all_gather x1, blocking collectives, on_device(): near = lax.all_gather(white, 'yl')  13 us
    ppermute x1, waiting for transfers between devices, on_device(): here = lax.ppermute(near, AXES, spread_pairs())  9.14 us
    ppermute x11, waiting for transfers between devices, ring(): return lax.ppermute(value, axis, [(i, (i + by) % n) for i in range(n)])  8.68 us
    ppermute x1, starting transfers between devices, on_device(): here = lax.ppermute(near, AXES, spread_pairs())  6.57 us
    pallas_call x1, Pallas kernels, whiten(): pl.pallas_call(whiten_kernel, in_specs=[anywhere, anywhere], out_specs=pl...  6.1 us
    pallas_call x1, Pallas kernels, cross(): pl.pallas_call(cross_kernel, in_specs=[pl.BlockSpec(memory_space=pltpu.SM...  3.92 us
  transfers between devices with their start and end apart: 12, of which 5 were waited for; matrix products, arithmetic and copies ran while one was open for 1% of the time, Pallas kernels for 0%

profile of v3, /device:TPU:19, one launch (start us, length us, event | category | flops | bytes accessed | tf_op | source)
XLA Modules:
  0.0 106.0 jit_solution(10946228980686901376)
XLA Ops:
  0.0 6.1 %whiten.1 = bf16[16,8,512]{2,1,0:T(8,128)(2,1)} custom-call(bf16[2048,512]{1,0:T(8,128)(2,1)} %bitcast.9, bf16[64,512]{1,0:T(8,128)(2,1)} %constant.41.clone.dft_ref), custom_call_target="tpu_custom_call" | custom-call | flops 3000000000 | bytes 3145728 | tf_op jit(solution)/shard_map/whiten/pallas_call | solution.py:97
  6.1 13.0 %all-gather = bf16[64,8,512]{2,1,0:T(8,128)(2,1)S(1)} all-gather(bf16[16,8,512]{2,1,0:T(8,128)(2,1)} %whiten.1), channel_id=2, replica_groups=mesh['z'=8,'yh'=2,'core'=2,'x'=4,'yl'=4] {'yl'}, dimensions={0}, use_global_device_ids=true | all-gather | bytes 655360 | tf_op jit(solution)/shard_map/all_gather | solution.py:242
  19.1 6.6 %collective-permute-start.3 = (bf16[4,16,8,512]{3,2,1,0:T(8,128)(2,1)S(1)}, bf16[4,16,8,512]{3,2,1,0:T(8,128)(2,1)S(1)}, u32[]{:S(2)}, u32[]{:S(2)}) collective-permute-start(bf16[4,16,8,512]{3,2,1,0:T(8,128)(2,1)S(1)} %bitcast.4), channel_id=1, source_target_pairs={{0,0},{16,16},{1,256},{17,272},{2,32},{18,48},{3,288},{19,304},{4,... | collective-permute-start | bytes 1572872 | tf_op jit(solution)/shard_map/ppermute | solution.py:243
  25.7 9.1 %collective-permute-done.3.refs_4_ = bf16[4,16,8,512]{3,2,1,0:T(8,128)(2,1)S(1)} collective-permute-done((bf16[4,16,8,512]{3,2,1,0:T(8,128)(2,1)S(1)}, bf16[4,16,8,512]{3,2,1,0:T(8,128)(2,1)S(1)}, u32[]{:S(2)}, u32[]{:S(2)}) %collective-permute-start.3) | collective-permute-done | bytes 524320 | tf_op jit(solution)/shard_map/ppermute | solution.py:243
  34.8 10.8 %collective-permute-start.4 = (bf16[4,16,8,512]{3,2,1,0:T(8,128)(2,1)S(1)}, bf16[4,16,8,512]{3,2,1,0:T(8,128)(2,1)S(1)}, u32[]{:S(2)}, u32[]{:S(2)}) collective-permute-start(bf16[4,16,8,512]{3,2,1,0:T(8,128)(2,1)S(1)} %collective-permute-done.3.refs_4_), channel_id=1, source_target_pairs={{0,64},{64,128},{128,192},{192,256},{256,320},{320,384},{384,448},... | collective-permute-start | bytes 1572872 | tf_op jit(solution)/shard_map/ppermute | solution.py:216
  45.7 22.0 %collective-permute-start.5 = (bf16[4,16,8,512]{3,2,1,0:T(8,128)(2,1)S(1)}, bf16[4,16,8,512]{3,2,1,0:T(8,128)(2,1)S(1)}, u32[]{:S(2)}, u32[]{:S(2)}) collective-permute-start(bf16[4,16,8,512]{3,2,1,0:T(8,128)(2,1)S(1)} %collective-permute-done.3.refs_4_), channel_id=1, source_target_pairs={{0,448},{64,0},{128,64},{192,128},{256,192},{320,256},{384,320},{4... | collective-permute-start | bytes 1572872 | tf_op jit(solution)/shard_map/ppermute | solution.py:216
  67.7 1.9 %collective-permute-start.2 = (bf16[4,16,8,512]{3,2,1,0:T(8,128)(2,1)S(1)}, bf16[4,16,8,512]{3,2,1,0:T(8,128)(2,1)S(1)}, u32[]{:S(2)}, u32[]{:S(2)}) collective-permute-start(bf16[4,16,8,512]{3,2,1,0:T(8,128)(2,1)S(1)} %bitcast.5), channel_id=1, source_target_pairs={{0,8},{4,12},{8,0},{12,4},{1,9},{5,13},{9,1},{13,5},{2,10},{6,14},... | collective-permute-start | bytes 1572872 | tf_op jit(solution)/shard_map/ppermute | solution.py:216
  69.6 1.9 %collective-permute-start.1 = (bf16[4,16,8,512]{3,2,1,0:T(8,128)(2,1)S(1)}, bf16[4,16,8,512]{3,2,1,0:T(8,128)(2,1)S(1)}, u32[]{:S(2)}, u32[]{:S(2)}) collective-permute-start(bf16[4,16,8,512]{3,2,1,0:T(8,128)(2,1)S(1)} %bitcast.6), channel_id=1, source_target_pairs={{0,12},{4,0},{8,4},{12,8},{1,13},{5,1},{9,5},{13,9},{2,14},{6,2},{... | collective-permute-start | bytes 1572872 | tf_op jit(solution)/shard_map/ppermute | solution.py:216
  71.5 5.9 %collective-permute-done.4.refs_5_ = bf16[4,16,8,512]{3,2,1,0:T(8,128)(2,1)S(1)} collective-permute-done((bf16[4,16,8,512]{3,2,1,0:T(8,128)(2,1)S(1)}, bf16[4,16,8,512]{3,2,1,0:T(8,128)(2,1)S(1)}, u32[]{:S(2)}, u32[]{:S(2)}) %collective-permute-start.4) | collective-permute-done | bytes 524320 | tf_op jit(solution)/shard_map/ppermute | solution.py:216
  77.4 1.9 %collective-permute-start.6 = (bf16[2,16,8,512]{3,2,1,0:T(8,128)(2,1)S(1)}, bf16[2,16,8,512]{3,2,1,0:T(8,128)(2,1)S(1)}, u32[]{:S(2)}, u32[]{:S(2)}) collective-permute-start(bf16[2,16,8,512]{3,2,1,0:T(8,128)(2,1)S(1)} %slice.8), channel_id=1, source_target_pairs={{0,64},{64,128},{128,192},{192,256},{256,320},{320,384},{384,448},... | collective-permute-start | bytes 786440 | tf_op jit(solution)/shard_map/ppermute | solution.py:216
  79.3 0.0 collective-permute-done.5.refs_6_
  79.4 4.6 %collective-permute-start.7 = (bf16[2,16,8,512]{3,2,1,0:T(8,128)(2,1)S(1)}, bf16[2,16,8,512]{3,2,1,0:T(8,128)(2,1)S(1)}, u32[]{:S(2)}, u32[]{:S(2)}) collective-permute-start(bf16[2,16,8,512]{3,2,1,0:T(8,128)(2,1)S(1)} %slice.9), channel_id=1, source_target_pairs={{0,448},{64,0},{128,64},{192,128},{256,192},{320,256},{384,320},{4... | collective-permute-start | bytes 786440 | tf_op jit(solution)/shard_map/ppermute | solution.py:216
  83.9 1.9 %collective-permute-start = (bf16[4,16,8,512]{3,2,1,0:T(8,128)(2,1)S(1)}, bf16[4,16,8,512]{3,2,1,0:T(8,128)(2,1)}, u32[]{:S(2)}, u32[]{:S(2)}) collective-permute-start(bf16[4,16,8,512]{3,2,1,0:T(8,128)(2,1)S(1)} %bitcast.7), channel_id=1, source_target_pairs={{0,4},{4,8},{8,12},{12,0},{1,5},{5,9},{9,13},{13,1},{2,6},{6,10},{... | collective-permute-start | bytes 1572872 | tf_op jit(solution)/shard_map/ppermute | solution.py:216
  85.9 1.2 %collective-permute-done.6 = bf16[2,16,8,512]{3,2,1,0:T(8,128)(2,1)S(1)} collective-permute-done((bf16[2,16,8,512]{3,2,1,0:T(8,128)(2,1)S(1)}, bf16[2,16,8,512]{3,2,1,0:T(8,128)(2,1)S(1)}, u32[]{:S(2)}, u32[]{:S(2)}) %collective-permute-start.6) | collective-permute-done | bytes 262176 | tf_op jit(solution)/shard_map/ppermute | solution.py:216
  87.1 4.0 %collective-permute-start.8 = (bf16[4,16,8,512]{3,2,1,0:T(8,128)(2,1)S(1)}, bf16[4,16,8,512]{3,2,1,0:T(8,128)(2,1)}, u32[]{:S(2)}, u32[]{:S(2)}) collective-permute-start(bf16[4,16,8,512]{3,2,1,0:T(8,128)(2,1)S(1)} %collective-permute-done.3.refs_4_), channel_id=1, source_target_pairs={{0,16},{16,0},{1,17},{17,1},{2,18},{18,2},{3,19},{19,3},{4,20},{20... | collective-permute-start | bytes 1572872 | tf_op jit(solution)/shard_map/ppermute | solution.py:216
  91.2 1.9 %collective-permute-start.10 = (bf16[4,16,8,512]{3,2,1,0:T(8,128)(2,1)S(1)}, bf16[4,16,8,512]{3,2,1,0:T(8,128)(2,1)}, u32[]{:S(2)}, u32[]{:S(2)}) collective-permute-start(bf16[4,16,8,512]{3,2,1,0:T(8,128)(2,1)S(1)} %collective-permute-done.5.refs_6_), channel_id=1, source_target_pairs={{0,16},{16,0},{1,17},{17,1},{2,18},{18,2},{3,19},{19,3},{4,20},{20... | collective-permute-start | bytes 1572872 | tf_op jit(solution)/shard_map/ppermute | solution.py:216
  93.1 2.4 %collective-permute-start.9 = (bf16[4,16,8,512]{3,2,1,0:T(8,128)(2,1)S(1)}, bf16[4,16,8,512]{3,2,1,0:T(8,128)(2,1)}, u32[]{:S(2)}, u32[]{:S(2)}) collective-permute-start(bf16[4,16,8,512]{3,2,1,0:T(8,128)(2,1)S(1)} %collective-permute-done.4.refs_5_), channel_id=1, source_target_pairs={{0,16},{16,0},{1,17},{17,1},{2,18},{18,2},{3,19},{19,3},{4,20},{20... | collective-permute-start | bytes 1572872 | tf_op jit(solution)/shard_map/ppermute | solution.py:216
  95.6 0.7 collective-permute-done.1.refs_2_
  96.3 0.8 copy-done
  97.0 2.3 %collective-permute-start.11 = (bf16[4,16,8,512]{3,2,1,0:T(8,128)(2,1)S(1)}, bf16[4,16,8,512]{3,2,1,0:T(8,128)(2,1)}, u32[]{:S(2)}, u32[]{:S(2)}) collective-permute-start(bf16[4,16,8,512]{3,2,1,0:T(8,128)(2,1)S(1)} %constant_dynamic-update-slice_fusion.refs_7_), channel_id=1, source_target_pairs={{0,16},{16,0},{1,17},{17,1},{2,18},{18,2},{3,19},{19,3},{4,20},{20... | collective-permute-start | bytes 1572872 | tf_op jit(solution)/shard_map/ppermute | solution.py:216
  99.4 0.7 dynamic-slice_bitcast_fusion.place_ref
  100.1 0.9 collective-permute-done.11.refs_11_
  101.0 1.0 copy-done.1
  102.0 3.9 %cross.1 = bf16[2,16,128,256]{3,2,1,0:T(8,128)(2,1)} custom-call(s32[12]{0:T(128)S(1)} %dynamic-slice_bitcast_fusion.place_ref, bf16[4,16,8,512]{3,2,1,0:T(8,128)(2,1)S(1)} %bitcast.8, bf16[4,16,8,512]{3,2,1,0:T(8,128)(2,1)} %collective-permute-done.refs_1_, bf16[4,16,8,512]{3,2,1,0:T(8,128)(2,1)S(1)} %copy-done.1, ...), custom_call_target="tpu_custom_call" | custom-call | flops 1100000000 | bytes 8388608 | tf_op jit(solution)/shard_map/cross/pallas_call | solution.py:155
  (12 shorter events, 0.1 us)
Async XLA Ops:
  19.1 15.7 %collective-permute-start.3 = (bf16[4,16,8,512]{3,2,1,0:T(8,128)(2,1)S(1)}, bf16[4,16,8,512]{3,2,1,0:T(8,128)(2,1)S(1)}, u32[]{:S(2)}, u32[]{:S(2)}) collective-permute-start(bf16[4,16,8,512]{3,2,1,0:T(8,128)(2,1)S(1)} %bitcast.4), channel_id=1, source_target_pairs={{0,0},{16,16},{1,256},{17,272},{2,32},{18,48},{3,288},{19,304},{4,... | collective-permute-start | bytes 1572872 | tf_op jit(solution)/shard_map/ppermute | solution.py:243
  34.8 42.5 %collective-permute-start.4 = (bf16[4,16,8,512]{3,2,1,0:T(8,128)(2,1)S(1)}, bf16[4,16,8,512]{3,2,1,0:T(8,128)(2,1)S(1)}, u32[]{:S(2)}, u32[]{:S(2)}) collective-permute-start(bf16[4,16,8,512]{3,2,1,0:T(8,128)(2,1)S(1)} %collective-permute-done.3.refs_4_), channel_id=1, source_target_pairs={{0,64},{64,128},{128,192},{192,256},{256,320},{320,384},{384,448},... | collective-permute-start | bytes 1572872 | tf_op jit(solution)/shard_map/ppermute | solution.py:216
  45.7 33.7 %collective-permute-start.5 = (bf16[4,16,8,512]{3,2,1,0:T(8,128)(2,1)S(1)}, bf16[4,16,8,512]{3,2,1,0:T(8,128)(2,1)S(1)}, u32[]{:S(2)}, u32[]{:S(2)}) collective-permute-start(bf16[4,16,8,512]{3,2,1,0:T(8,128)(2,1)S(1)} %collective-permute-done.3.refs_4_), channel_id=1, source_target_pairs={{0,448},{64,0},{128,64},{192,128},{256,192},{320,256},{384,320},{4... | collective-permute-start | bytes 1572872 | tf_op jit(solution)/shard_map/ppermute | solution.py:216
  67.7 25.5 %collective-permute-start.2 = (bf16[4,16,8,512]{3,2,1,0:T(8,128)(2,1)S(1)}, bf16[4,16,8,512]{3,2,1,0:T(8,128)(2,1)S(1)}, u32[]{:S(2)}, u32[]{:S(2)}) collective-permute-start(bf16[4,16,8,512]{3,2,1,0:T(8,128)(2,1)S(1)} %bitcast.5), channel_id=1, source_target_pairs={{0,8},{4,12},{8,0},{12,4},{1,9},{5,13},{9,1},{13,5},{2,10},{6,14},... | collective-permute-start | bytes 1572872 | tf_op jit(solution)/shard_map/ppermute | solution.py:216
  69.6 26.7 %collective-permute-start.1 = (bf16[4,16,8,512]{3,2,1,0:T(8,128)(2,1)S(1)}, bf16[4,16,8,512]{3,2,1,0:T(8,128)(2,1)S(1)}, u32[]{:S(2)}, u32[]{:S(2)}) collective-permute-start(bf16[4,16,8,512]{3,2,1,0:T(8,128)(2,1)S(1)} %bitcast.6), channel_id=1, source_target_pairs={{0,12},{4,0},{8,4},{12,8},{1,13},{5,1},{9,5},{13,9},{2,14},{6,2},{... | collective-permute-start | bytes 1572872 | tf_op jit(solution)/shard_map/ppermute | solution.py:216
  77.4 9.7 %collective-permute-start.6 = (bf16[2,16,8,512]{3,2,1,0:T(8,128)(2,1)S(1)}, bf16[2,16,8,512]{3,2,1,0:T(8,128)(2,1)S(1)}, u32[]{:S(2)}, u32[]{:S(2)}) collective-permute-start(bf16[2,16,8,512]{3,2,1,0:T(8,128)(2,1)S(1)} %slice.8), channel_id=1, source_target_pairs={{0,64},{64,128},{128,192},{192,256},{256,320},{320,384},{384,448},... | collective-permute-start | bytes 786440 | tf_op jit(solution)/shard_map/ppermute | solution.py:216
  79.4 11.8 %collective-permute-start.7 = (bf16[2,16,8,512]{3,2,1,0:T(8,128)(2,1)S(1)}, bf16[2,16,8,512]{3,2,1,0:T(8,128)(2,1)S(1)}, u32[]{:S(2)}, u32[]{:S(2)}) collective-permute-start(bf16[2,16,8,512]{3,2,1,0:T(8,128)(2,1)S(1)} %slice.9), channel_id=1, source_target_pairs={{0,448},{64,0},{128,64},{192,128},{256,192},{320,256},{384,320},{4... | collective-permute-start | bytes 786440 | tf_op jit(solution)/shard_map/ppermute | solution.py:216
  83.9 16.1 %collective-permute-start = (bf16[4,16,8,512]{3,2,1,0:T(8,128)(2,1)S(1)}, bf16[4,16,8,512]{3,2,1,0:T(8,128)(2,1)}, u32[]{:S(2)}, u32[]{:S(2)}) collective-permute-start(bf16[4,16,8,512]{3,2,1,0:T(8,128)(2,1)S(1)} %bitcast.7), channel_id=1, source_target_pairs={{0,4},{4,8},{8,12},{12,0},{1,5},{5,9},{9,13},{13,1},{2,6},{6,10},{... | collective-permute-start | bytes 1572872 | tf_op jit(solution)/shard_map/ppermute | solution.py:216
  87.1 13.0 %collective-permute-start.8 = (bf16[4,16,8,512]{3,2,1,0:T(8,128)(2,1)S(1)}, bf16[4,16,8,512]{3,2,1,0:T(8,128)(2,1)}, u32[]{:S(2)}, u32[]{:S(2)}) collective-permute-start(bf16[4,16,8,512]{3,2,1,0:T(8,128)(2,1)S(1)} %collective-permute-done.3.refs_4_), channel_id=1, source_target_pairs={{0,16},{16,0},{1,17},{17,1},{2,18},{18,2},{3,19},{19,3},{4,20},{20... | collective-permute-start | bytes 1572872 | tf_op jit(solution)/shard_map/ppermute | solution.py:216
  91.2 8.9 %collective-permute-start.10 = (bf16[4,16,8,512]{3,2,1,0:T(8,128)(2,1)S(1)}, bf16[4,16,8,512]{3,2,1,0:T(8,128)(2,1)}, u32[]{:S(2)}, u32[]{:S(2)}) collective-permute-start(bf16[4,16,8,512]{3,2,1,0:T(8,128)(2,1)S(1)} %collective-permute-done.5.refs_6_), channel_id=1, source_target_pairs={{0,16},{16,0},{1,17},{17,1},{2,18},{18,2},{3,19},{19,3},{4,20},{20... | collective-permute-start | bytes 1572872 | tf_op jit(solution)/shard_map/ppermute | solution.py:216
  93.1 6.9 %collective-permute-start.9 = (bf16[4,16,8,512]{3,2,1,0:T(8,128)(2,1)S(1)}, bf16[4,16,8,512]{3,2,1,0:T(8,128)(2,1)}, u32[]{:S(2)}, u32[]{:S(2)}) collective-permute-start(bf16[4,16,8,512]{3,2,1,0:T(8,128)(2,1)S(1)} %collective-permute-done.4.refs_5_), channel_id=1, source_target_pairs={{0,16},{16,0},{1,17},{17,1},{2,18},{18,2},{3,19},{19,3},{4,20},{20... | collective-permute-start | bytes 1572872 | tf_op jit(solution)/shard_map/ppermute | solution.py:216
  96.3 0.8 copy-start
  97.0 3.9 %collective-permute-start.11 = (bf16[4,16,8,512]{3,2,1,0:T(8,128)(2,1)S(1)}, bf16[4,16,8,512]{3,2,1,0:T(8,128)(2,1)}, u32[]{:S(2)}, u32[]{:S(2)}) collective-permute-start(bf16[4,16,8,512]{3,2,1,0:T(8,128)(2,1)S(1)} %constant_dynamic-update-slice_fusion.refs_7_), channel_id=1, source_target_pairs={{0,16},{16,0},{1,17},{17,1},{2,18},{18,2},{3,19},{19,3},{4,20},{20... | collective-permute-start | bytes 1572872 | tf_op jit(solution)/shard_map/ppermute | solution.py:216
  101.0 1.0 copy-start.1

commit v4 on v3

--- a/solution.py
+++ b/solution.py
@@ -127,9 +127,10 @@
     out_ref, left_ref, right_ref, tile_ref, out_sem = refs[count:]
 
     def gather(b):
-        for k, piece in enumerate(pieces):
-            target = left_ref if k < 4 else right_ref
-            target[b, place_ref[k]] = piece[:, b]
+        for k in range(4):
+            left_ref[b, k] = pieces[0][4 * k : 4 * k + 4, b]
+        for k, piece in enumerate(pieces[1:]):
+            right_ref[b, place_ref[4 + k]] = piece[:, b]
 
     gather(0)
     outs = []
@@ -241,7 +242,8 @@
     white = whiten(raw)
     near = lax.all_gather(white, "yl")
     here = lax.ppermute(near, AXES, spread_pairs())
-    rows = [near] + [ring(near, "x", by) for by in (1, -1, 2)]
+    rows = lax.all_to_all(jnp.broadcast_to(near[None], (4,) + near.shape), "x", 0, 0)
+    rows = [rows.reshape((16,) + white.shape)]
     below = ring(here, "z", 1)
     above = ring(here, "z", -1)
     far = jnp.concatenate([ring(below[:2], "z", 1), ring(above[2:], "z", -1)])

time: 106 us -> 103 us (0.972)
  the two profiles are of different devices: /device:TPU:19 before, /device:TPU:35 now
where the time goes in v4:
time: 103 us; the launch traced here: 102 us
  starting transfers between devices  64.1 us (62%)
  blocking collectives  12.4 us (12%)
  waiting for transfers between devices  11.6 us (11%)
  Pallas kernels  10.1 us (10%)
  local copies, waits for them, and re-layouts  3.7 us (4%)
    ppermute x8, starting transfers between devices, ring(): return lax.ppermute(value, axis, [(i, (i + by) % n) for i in range(n)])  52.4 us
    all_gather x1, blocking collectives, on_device(): near = lax.all_gather(white, 'yl')  12.4 us
    ppermute x8, waiting for transfers between devices, ring(): return lax.ppermute(value, axis, [(i, (i + by) % n) for i in range(n)])  9.91 us
    all_to_all x1, starting transfers between devices, on_device(): lax.all_to_all(jnp.broadcast_to(near[None], (4,) + near.shape), 'x', 0, 0)  7.56 us
    pallas_call x1, Pallas kernels, whiten(): pl.pallas_call(whiten_kernel, in_specs=[anywhere, anywhere], out_specs=pl...  6.09 us
    ppermute x1, starting transfers between devices, on_device(): here = lax.ppermute(near, AXES, spread_pairs())  4.1 us
    pallas_call x1, Pallas kernels, cross(): pl.pallas_call(cross_kernel, in_specs=[pl.BlockSpec(memory_space=pltpu.SM...  4.04 us
  transfers between devices with their start and end apart: 10, of which 3 were waited for; matrix products, arithmetic and copies ran while one was open for 4% of the time, Pallas kernels for 0%

profile of v4, /device:TPU:35, one launch (start us, length us, event | category | flops | bytes accessed | tf_op | source)
XLA Modules:
  0.0 102.0 jit_solution(5133000291974998014)
XLA Ops:
  0.0 6.1 %whiten.1 = bf16[16,8,512]{2,1,0:T(8,128)(2,1)} custom-call(bf16[2048,512]{1,0:T(8,128)(2,1)} %bitcast.8, bf16[64,512]{1,0:T(8,128)(2,1)} %constant.41.clone.dft_ref), custom_call_target="tpu_custom_call" | custom-call | flops 3000000000 | bytes 3145728 | tf_op jit(solution)/shard_map/whiten/pallas_call | solution.py:97
  6.1 12.4 %all-gather = bf16[64,8,512]{2,1,0:T(8,128)(2,1)S(1)} all-gather(bf16[16,8,512]{2,1,0:T(8,128)(2,1)} %whiten.1), channel_id=2, replica_groups=mesh['z'=8,'yh'=2,'core'=2,'x'=4,'yl'=4] {'yl'}, dimensions={0}, use_global_device_ids=true | all-gather | bytes 655360 | tf_op jit(solution)/shard_map/all_gather | solution.py:243
  18.5 4.1 %collective-permute-start = (bf16[4,16,8,512]{3,2,1,0:T(8,128)(2,1)S(1)}, bf16[4,16,8,512]{3,2,1,0:T(8,128)(2,1)}, u32[]{:S(2)}, u32[]{:S(2)}) collective-permute-start(bf16[4,16,8,512]{3,2,1,0:T(8,128)(2,1)S(1)} %bitcast.6), channel_id=1, source_target_pairs={{0,0},{16,16},{1,256},{17,272},{2,32},{18,48},{3,288},{19,304},{4,... | collective-permute-start | bytes 1572872 | tf_op jit(solution)/shard_map/ppermute | solution.py:244
  22.6 1.5 %broadcast_in_dim.2 = bf16[4,4,16,8,512]{4,3,2,1,0:T(8,128)(2,1)} broadcast(bf16[4,16,8,512]{3,2,1,0:T(8,128)(2,1)S(1)} %bitcast.7), dimensions={1,2,3,4} | broadcast | bytes 2621440 | tf_op jit(solution)/shard_map/broadcast_in_dim | solution.py:245
  24.1 7.6 %all-to-all-start = ((bf16[4,4,16,8,512]{4,3,2,1,0:T(8,128)(2,1)}), bf16[4,4,16,8,512]{4,3,2,1,0:T(8,128)(2,1)S(1)}, u32[]{:S(2)}, u32[]{:S(2)}) async-start(bf16[4,4,16,8,512]{4,3,2,1,0:T(8,128)(2,1)} %broadcast_in_dim.2), calls=%async_computation | async-start | bytes 4194304 | tf_op jit(solution)/shard_map/all_to_all | solution.py:245
  31.7 1.7 %collective-permute-done.refs_1_ = bf16[4,16,8,512]{3,2,1,0:T(8,128)(2,1)} collective-permute-done((bf16[4,16,8,512]{3,2,1,0:T(8,128)(2,1)S(1)}, bf16[4,16,8,512]{3,2,1,0:T(8,128)(2,1)}, u32[]{:S(2)}, u32[]{:S(2)}) %collective-permute-start) | collective-permute-done | bytes 524320 | tf_op jit(solution)/shard_map/ppermute | solution.py:244
  33.3 4.0 %collective-permute-start.1 = (bf16[4,16,8,512]{3,2,1,0:T(8,128)(2,1)}, bf16[4,16,8,512]{3,2,1,0:T(8,128)(2,1)S(1)}, u32[]{:S(2)}, u32[]{:S(2)}) collective-permute-start(bf16[4,16,8,512]{3,2,1,0:T(8,128)(2,1)} %collective-permute-done.refs_1_), channel_id=1, source_target_pairs={{0,64},{64,128},{128,192},{192,256},{256,320},{320,384},{384,448},... | collective-permute-start | bytes 1572872 | tf_op jit(solution)/shard_map/ppermute | solution.py:217
  37.3 21.5 %collective-permute-start.2 = (bf16[4,16,8,512]{3,2,1,0:T(8,128)(2,1)}, bf16[4,16,8,512]{3,2,1,0:T(8,128)(2,1)S(1)}, u32[]{:S(2)}, u32[]{:S(2)}) collective-permute-start(bf16[4,16,8,512]{3,2,1,0:T(8,128)(2,1)} %collective-permute-done.refs_1_), channel_id=1, source_target_pairs={{0,448},{64,0},{128,64},{192,128},{256,192},{320,256},{384,320},{4... | collective-permute-start | bytes 1572872 | tf_op jit(solution)/shard_map/ppermute | solution.py:217
  58.8 8.4 %collective-permute-done.1.refs_2_ = bf16[4,16,8,512]{3,2,1,0:T(8,128)(2,1)S(1)} collective-permute-done((bf16[4,16,8,512]{3,2,1,0:T(8,128)(2,1)}, bf16[4,16,8,512]{3,2,1,0:T(8,128)(2,1)S(1)}, u32[]{:S(2)}, u32[]{:S(2)}) %collective-permute-start.1) | collective-permute-done | bytes 524320 | tf_op jit(solution)/shard_map/ppermute | solution.py:217
  67.3 1.9 %collective-permute-start.3 = (bf16[2,16,8,512]{3,2,1,0:T(8,128)(2,1)S(1)}, bf16[2,16,8,512]{3,2,1,0:T(8,128)(2,1)S(1)}, u32[]{:S(2)}, u32[]{:S(2)}) collective-permute-start(bf16[2,16,8,512]{3,2,1,0:T(8,128)(2,1)S(1)} %slice.8), channel_id=1, source_target_pairs={{0,64},{64,128},{128,192},{192,256},{256,320},{320,384},{384,448},... | collective-permute-start | bytes 786440 | tf_op jit(solution)/shard_map/ppermute | solution.py:217
  69.2 0.0 collective-permute-done.2.refs_3_
  69.2 15.2 %collective-permute-start.4 = (bf16[2,16,8,512]{3,2,1,0:T(8,128)(2,1)S(1)}, bf16[2,16,8,512]{3,2,1,0:T(8,128)(2,1)S(1)}, u32[]{:S(2)}, u32[]{:S(2)}) collective-permute-start(bf16[2,16,8,512]{3,2,1,0:T(8,128)(2,1)S(1)} %slice.9), channel_id=1, source_target_pairs={{0,448},{64,0},{128,64},{192,128},{256,192},{320,256},{384,320},{4... | collective-permute-start | bytes 786440 | tf_op jit(solution)/shard_map/ppermute | solution.py:217
  84.5 3.6 %collective-permute-start.5 = (bf16[4,16,8,512]{3,2,1,0:T(8,128)(2,1)}, bf16[4,16,8,512]{3,2,1,0:T(8,128)(2,1)}, u32[]{:S(2)}, u32[]{:S(2)}) collective-permute-start(bf16[4,16,8,512]{3,2,1,0:T(8,128)(2,1)} %collective-permute-done.refs_1_), channel_id=1, source_target_pairs={{0,16},{16,0},{1,17},{17,1},{2,18},{18,2},{3,19},{19,3},{4,20},{20... | collective-permute-start | bytes 1572872 | tf_op jit(solution)/shard_map/ppermute | solution.py:217
  88.1 1.9 %collective-permute-start.6 = (bf16[4,16,8,512]{3,2,1,0:T(8,128)(2,1)S(1)}, bf16[4,16,8,512]{3,2,1,0:T(8,128)(2,1)}, u32[]{:S(2)}, u32[]{:S(2)}) collective-permute-start(bf16[4,16,8,512]{3,2,1,0:T(8,128)(2,1)S(1)} %collective-permute-done.1.refs_2_), channel_id=1, source_target_pairs={{0,16},{16,0},{1,17},{17,1},{2,18},{18,2},{3,19},{19,3},{4,20},{20... | collective-permute-start | bytes 1572872 | tf_op jit(solution)/shard_map/ppermute | solution.py:217
  90.0 2.4 %collective-permute-start.7 = (bf16[4,16,8,512]{3,2,1,0:T(8,128)(2,1)S(1)}, bf16[4,16,8,512]{3,2,1,0:T(8,128)(2,1)}, u32[]{:S(2)}, u32[]{:S(2)}) collective-permute-start(bf16[4,16,8,512]{3,2,1,0:T(8,128)(2,1)S(1)} %collective-permute-done.2.refs_3_), channel_id=1, source_target_pairs={{0,16},{16,0},{1,17},{17,1},{2,18},{18,2},{3,19},{19,3},{4,20},{20... | collective-permute-start | bytes 1572872 | tf_op jit(solution)/shard_map/ppermute | solution.py:217
  92.4 0.0 collective-permute-done.3
  92.4 0.7 constant_dynamic-update-slice_fusion.1
  93.1 0.0 collective-permute-done.4
  93.1 0.7 constant_dynamic-update-slice_fusion.refs_4_
  93.9 1.9 %collective-permute-start.8 = (bf16[4,16,8,512]{3,2,1,0:T(8,128)(2,1)}, bf16[4,16,8,512]{3,2,1,0:T(8,128)(2,1)}, u32[]{:S(2)}, u32[]{:S(2)}) collective-permute-start(bf16[4,16,8,512]{3,2,1,0:T(8,128)(2,1)} %constant_dynamic-update-slice_fusion.refs_4_), channel_id=1, source_target_pairs={{0,16},{16,0},{1,17},{17,1},{2,18},{18,2},{3,19},{19,3},{4,20},{20... | collective-permute-start | bytes 1572872 | tf_op jit(solution)/shard_map/ppermute | solution.py:217
  95.8 0.7 dynamic-slice_bitcast_fusion.place_ref
  96.5 0.0 collective-permute-done.5.refs_5_
  96.5 1.5 %collective-permute-done.8.refs_8_ = bf16[4,16,8,512]{3,2,1,0:T(8,128)(2,1)} collective-permute-done((bf16[4,16,8,512]{3,2,1,0:T(8,128)(2,1)}, bf16[4,16,8,512]{3,2,1,0:T(8,128)(2,1)}, u32[]{:S(2)}, u32[]{:S(2)}) %collective-permute-start.8) | collective-permute-done | bytes 524320 | tf_op jit(solution)/shard_map/ppermute | solution.py:217
  98.0 4.0 %cross.1 = bf16[2,16,128,256]{3,2,1,0:T(8,128)(2,1)} custom-call(s32[12]{0:T(128)S(1)} %dynamic-slice_bitcast_fusion.place_ref, bf16[16,16,8,512]{3,2,1,0:T(8,128)(2,1)S(1)} %bitcast.5, bf16[4,16,8,512]{3,2,1,0:T(8,128)(2,1)} %collective-permute-done.refs_1_, bf16[4,16,8,512]{3,2,1,0:T(8,128)(2,1)S(1)} %collective-permute-done.1.refs_2_, ...), custom_call_target="tpu_custom_call" | custom-call | flops 1100000000 | bytes 8388608 | tf_op jit(solution)/shard_map/cross/pallas_call | solution.py:156
  (5 shorter events, 0.0 us)
Async XLA Ops:
  18.5 14.8 %collective-permute-start = (bf16[4,16,8,512]{3,2,1,0:T(8,128)(2,1)S(1)}, bf16[4,16,8,512]{3,2,1,0:T(8,128)(2,1)}, u32[]{:S(2)}, u32[]{:S(2)}) collective-permute-start(bf16[4,16,8,512]{3,2,1,0:T(8,128)(2,1)S(1)} %bitcast.6), channel_id=1, source_target_pairs={{0,0},{16,16},{1,256},{17,272},{2,32},{18,48},{3,288},{19,304},{4,... | collective-permute-start | bytes 1572872 | tf_op jit(solution)/shard_map/ppermute | solution.py:244
  24.1 72.4 %all-to-all-start = ((bf16[4,4,16,8,512]{4,3,2,1,0:T(8,128)(2,1)}), bf16[4,4,16,8,512]{4,3,2,1,0:T(8,128)(2,1)S(1)}, u32[]{:S(2)}, u32[]{:S(2)}) async-start(bf16[4,4,16,8,512]{4,3,2,1,0:T(8,128)(2,1)} %broadcast_in_dim.2), calls=%async_computation | async-start | bytes 4194304 | tf_op jit(solution)/shard_map/all_to_all | solution.py:245
  33.3 33.9 %collective-permute-start.1 = (bf16[4,16,8,512]{3,2,1,0:T(8,128)(2,1)}, bf16[4,16,8,512]{3,2,1,0:T(8,128)(2,1)S(1)}, u32[]{:S(2)}, u32[]{:S(2)}) collective-permute-start(bf16[4,16,8,512]{3,2,1,0:T(8,128)(2,1)} %collective-permute-done.refs_1_), channel_id=1, source_target_pairs={{0,64},{64,128},{128,192},{192,256},{256,320},{320,384},{384,448},... | collective-permute-start | bytes 1572872 | tf_op jit(solution)/shard_map/ppermute | solution.py:217
  37.3 31.9 %collective-permute-start.2 = (bf16[4,16,8,512]{3,2,1,0:T(8,128)(2,1)}, bf16[4,16,8,512]{3,2,1,0:T(8,128)(2,1)S(1)}, u32[]{:S(2)}, u32[]{:S(2)}) collective-permute-start(bf16[4,16,8,512]{3,2,1,0:T(8,128)(2,1)} %collective-permute-done.refs_1_), channel_id=1, source_target_pairs={{0,448},{64,0},{128,64},{192,128},{256,192},{320,256},{384,320},{4... | collective-permute-start | bytes 1572872 | tf_op jit(solution)/shard_map/ppermute | solution.py:217
  67.3 25.1 %collective-permute-start.3 = (bf16[2,16,8,512]{3,2,1,0:T(8,128)(2,1)S(1)}, bf16[2,16,8,512]{3,2,1,0:T(8,128)(2,1)S(1)}, u32[]{:S(2)}, u32[]{:S(2)}) collective-permute-start(bf16[2,16,8,512]{3,2,1,0:T(8,128)(2,1)S(1)} %slice.8), channel_id=1, source_target_pairs={{0,64},{64,128},{128,192},{192,256},{256,320},{320,384},{384,448},... | collective-permute-start | bytes 786440 | tf_op jit(solution)/shard_map/ppermute | solution.py:217
  69.2 23.9 %collective-permute-start.4 = (bf16[2,16,8,512]{3,2,1,0:T(8,128)(2,1)S(1)}, bf16[2,16,8,512]{3,2,1,0:T(8,128)(2,1)S(1)}, u32[]{:S(2)}, u32[]{:S(2)}) collective-permute-start(bf16[2,16,8,512]{3,2,1,0:T(8,128)(2,1)S(1)} %slice.9), channel_id=1, source_target_pairs={{0,448},{64,0},{128,64},{192,128},{256,192},{320,256},{384,320},{4... | collective-permute-start | bytes 786440 | tf_op jit(solution)/shard_map/ppermute | solution.py:217
  84.5 12.0 %collective-permute-start.5 = (bf16[4,16,8,512]{3,2,1,0:T(8,128)(2,1)}, bf16[4,16,8,512]{3,2,1,0:T(8,128)(2,1)}, u32[]{:S(2)}, u32[]{:S(2)}) collective-permute-start(bf16[4,16,8,512]{3,2,1,0:T(8,128)(2,1)} %collective-permute-done.refs_1_), channel_id=1, source_target_pairs={{0,16},{16,0},{1,17},{17,1},{2,18},{18,2},{3,19},{19,3},{4,20},{20... | collective-permute-start | bytes 1572872 | tf_op jit(solution)/shard_map/ppermute | solution.py:217
  88.1 8.4 %collective-permute-start.6 = (bf16[4,16,8,512]{3,2,1,0:T(8,128)(2,1)S(1)}, bf16[4,16,8,512]{3,2,1,0:T(8,128)(2,1)}, u32[]{:S(2)}, u32[]{:S(2)}) collective-permute-start(bf16[4,16,8,512]{3,2,1,0:T(8,128)(2,1)S(1)} %collective-permute-done.1.refs_2_), channel_id=1, source_target_pairs={{0,16},{16,0},{1,17},{17,1},{2,18},{18,2},{3,19},{19,3},{4,20},{20... | collective-permute-start | bytes 1572872 | tf_op jit(solution)/shard_map/ppermute | solution.py:217
  90.0 6.5 %collective-permute-start.7 = (bf16[4,16,8,512]{3,2,1,0:T(8,128)(2,1)S(1)}, bf16[4,16,8,512]{3,2,1,0:T(8,128)(2,1)}, u32[]{:S(2)}, u32[]{:S(2)}) collective-permute-start(bf16[4,16,8,512]{3,2,1,0:T(8,128)(2,1)S(1)} %collective-permute-done.2.refs_3_), channel_id=1, source_target_pairs={{0,16},{16,0},{1,17},{17,1},{2,18},{18,2},{3,19},{19,3},{4,20},{20... | collective-permute-start | bytes 1572872 | tf_op jit(solution)/shard_map/ppermute | solution.py:217
  93.9 4.1 %collective-permute-start.8 = (bf16[4,16,8,512]{3,2,1,0:T(8,128)(2,1)}, bf16[4,16,8,512]{3,2,1,0:T(8,128)(2,1)}, u32[]{:S(2)}, u32[]{:S(2)}) collective-permute-start(bf16[4,16,8,512]{3,2,1,0:T(8,128)(2,1)} %constant_dynamic-update-slice_fusion.refs_4_), channel_id=1, source_target_pairs={{0,16},{16,0},{1,17},{17,1},{2,18},{18,2},{3,19},{19,3},{4,20},{20... | collective-permute-start | bytes 1572872 | tf_op jit(solution)/shard_map/ppermute | solution.py:217

commit v5 on v4

--- a/solution.py
+++ b/solution.py
@@ -54,8 +54,6 @@
     there = lax.broadcasted_iota(jnp.int32, (SAMPLES, SAMPLES), 1)
     near = jnp.abs(here - there) <= SPAN // 2
     band = jnp.where(near, 1.0, 0.0).astype(jnp.bfloat16)
-    table_copy.wait()
-    dft = table_ref[...]
     per_half = CHUNKS // 2
     for half in range(2):
         for part in range(per_half):
@@ -68,6 +66,9 @@
                 balanced_ref[lane, pl.ds(chunk * rows, rows), :] = balanced[
                     :, lane * 128 : (lane + 1) * 128
                 ]
+        if half == 0:
+            table_copy.wait()
+            dft = table_ref[...]
         first = half * HALF * 8
         for channel in range(8):
             balanced = jnp.concatenate(
@@ -122,13 +123,11 @@
 
 
 def cross_kernel(place_ref, *refs):
-    count = len(refs) - 5
+    count = len(refs) - 4
     pieces = refs[:count]
-    out_ref, left_ref, right_ref, tile_ref, out_sem = refs[count:]
+    out_ref, right_ref, tile_ref, out_sem = refs[count:]
 
     def gather(b):
-        for k in range(4):
-            left_ref[b, k] = pieces[0][4 * k : 4 * k + 4, b]
         for k, piece in enumerate(pieces[1:]):
             right_ref[b, place_ref[4 + k]] = piece[:, b]
 
@@ -137,7 +136,7 @@
     for b in range(BINS):
         if b + 1 < BINS:
             gather(b + 1)
-        left = left_ref[b].reshape(128, 2 * WINDOWS)
+        left = pieces[0][:, b].reshape(128, 2 * WINDOWS)
         right = right_ref[b].reshape(256, 2 * WINDOWS)
         tile_ref[0, b], tile_ref[1, b] = multiply(left, right)
         if b % GROUP == GROUP - 1:
@@ -160,12 +159,11 @@
         out_specs=pl.BlockSpec(memory_space=pl.ANY),
         out_shape=jax.ShapeDtypeStruct(out, jnp.bfloat16),
         scratch_shapes=[
-            pltpu.VMEM((BINS, 4, 4, 8, 2 * WINDOWS), jnp.bfloat16),
             pltpu.VMEM((BINS, 8, 4, 8, 2 * WINDOWS), jnp.bfloat16),
             pltpu.VMEM(out, jnp.bfloat16),
             pltpu.SemaphoreType.DMA((BINS // GROUP,)),
         ],
-        compiler_params=pltpu.CompilerParams(vmem_limit_bytes=40 << 20),
+        compiler_params=pltpu.CompilerParams(vmem_limit_bytes=20 << 20),
         cost_estimate=pl.CostEstimate(
             flops=1_100_000_000, bytes_accessed=8 << 20, transcendentals=0
         ),

time: 103 us -> 102 us (level)
  no operation moved by 1% of the time
where the time goes in v5:
time: 102 us
  starting transfers between devices  64 us (63%)
  blocking collectives  12.4 us (12%)
  waiting for transfers between devices  11.6 us (11%)
  Pallas kernels  9.69 us (10%)
  local copies, waits for them, and re-layouts  3.7 us (4%)
    ppermute x8, starting transfers between devices, ring(): return lax.ppermute(value, axis, [(i, (i + by) % n) for i in range(n)])  52.4 us
    all_gather x1, blocking collectives, on_device(): near = lax.all_gather(white, 'yl')  12.4 us
    ppermute x8, waiting for transfers between devices, ring(): return lax.ppermute(value, axis, [(i, (i + by) % n) for i in range(n)])  9.9 us
    all_to_all x1, starting transfers between devices, on_device(): lax.all_to_all(jnp.broadcast_to(near[None], (4,) + near.shape), 'x', 0, 0)  7.53 us
    pallas_call x1, Pallas kernels, whiten(): pl.pallas_call(whiten_kernel, in_specs=[anywhere, anywhere], out_specs=pl...  5.65 us
    ppermute x1, starting transfers between devices, on_device(): here = lax.ppermute(near, AXES, spread_pairs())  4.11 us
    pallas_call x1, Pallas kernels, cross(): pl.pallas_call(cross_kernel, in_specs=[pl.BlockSpec(memory_space=pltpu.SM...  4.04 us
  transfers between devices with their start and end apart: 10, of which 3 were waited for; matrix products, arithmetic and copies ran while one was open for 4% of the time, Pallas kernels for 0%

profile of v5, /device:TPU:35, one launch (start us, length us, event | category | flops | bytes accessed | tf_op | source)
XLA Modules:
  0.0 101.6 jit_solution(4397773785465834831)
XLA Ops:
  0.0 5.7 %whiten.1 = bf16[16,8,512]{2,1,0:T(8,128)(2,1)} custom-call(bf16[2048,512]{1,0:T(8,128)(2,1)} %bitcast.8, bf16[64,512]{1,0:T(8,128)(2,1)} %constant.41.clone.dft_ref), custom_call_target="tpu_custom_call" | custom-call | flops 3000000000 | bytes 3145728 | tf_op jit(solution)/shard_map/whiten/pallas_call | solution.py:98
  5.7 12.4 %all-gather = bf16[64,8,512]{2,1,0:T(8,128)(2,1)S(1)} all-gather(bf16[16,8,512]{2,1,0:T(8,128)(2,1)} %whiten.1), channel_id=2, replica_groups=mesh['z'=8,'yh'=2,'core'=2,'x'=4,'yl'=4] {'yl'}, dimensions={0}, use_global_device_ids=true | all-gather | bytes 655360 | tf_op jit(solution)/shard_map/all_gather | solution.py:241
  18.1 4.1 %collective-permute-start = (bf16[4,16,8,512]{3,2,1,0:T(8,128)(2,1)S(1)}, bf16[4,16,8,512]{3,2,1,0:T(8,128)(2,1)}, u32[]{:S(2)}, u32[]{:S(2)}) collective-permute-start(bf16[4,16,8,512]{3,2,1,0:T(8,128)(2,1)S(1)} %bitcast.6), channel_id=1, source_target_pairs={{0,0},{16,16},{1,256},{17,272},{2,32},{18,48},{3,288},{19,304},{4,... | collective-permute-start | bytes 1572872 | tf_op jit(solution)/shard_map/ppermute | solution.py:242
  22.2 1.5 %broadcast_in_dim.2 = bf16[4,4,16,8,512]{4,3,2,1,0:T(8,128)(2,1)} broadcast(bf16[4,16,8,512]{3,2,1,0:T(8,128)(2,1)S(1)} %bitcast.7), dimensions={1,2,3,4} | broadcast | bytes 2621440 | tf_op jit(solution)/shard_map/broadcast_in_dim | solution.py:243
  23.7 7.5 %all-to-all-start = ((bf16[4,4,16,8,512]{4,3,2,1,0:T(8,128)(2,1)}), bf16[4,4,16,8,512]{4,3,2,1,0:T(8,128)(2,1)S(1)}, u32[]{:S(2)}, u32[]{:S(2)}) async-start(bf16[4,4,16,8,512]{4,3,2,1,0:T(8,128)(2,1)} %broadcast_in_dim.2), calls=%async_computation | async-start | bytes 4194304 | tf_op jit(solution)/shard_map/all_to_all | solution.py:243
  31.2 1.7 %collective-permute-done.refs_1_ = bf16[4,16,8,512]{3,2,1,0:T(8,128)(2,1)} collective-permute-done((bf16[4,16,8,512]{3,2,1,0:T(8,128)(2,1)S(1)}, bf16[4,16,8,512]{3,2,1,0:T(8,128)(2,1)}, u32[]{:S(2)}, u32[]{:S(2)}) %collective-permute-start) | collective-permute-done | bytes 524320 | tf_op jit(solution)/shard_map/ppermute | solution.py:242
  32.9 4.0 %collective-permute-start.1 = (bf16[4,16,8,512]{3,2,1,0:T(8,128)(2,1)}, bf16[4,16,8,512]{3,2,1,0:T(8,128)(2,1)S(1)}, u32[]{:S(2)}, u32[]{:S(2)}) collective-permute-start(bf16[4,16,8,512]{3,2,1,0:T(8,128)(2,1)} %collective-permute-done.refs_1_), channel_id=1, source_target_pairs={{0,64},{64,128},{128,192},{192,256},{256,320},{320,384},{384,448},... | collective-permute-start | bytes 1572872 | tf_op jit(solution)/shard_map/ppermute | solution.py:215
  36.9 21.4 %collective-permute-start.2 = (bf16[4,16,8,512]{3,2,1,0:T(8,128)(2,1)}, bf16[4,16,8,512]{3,2,1,0:T(8,128)(2,1)S(1)}, u32[]{:S(2)}, u32[]{:S(2)}) collective-permute-start(bf16[4,16,8,512]{3,2,1,0:T(8,128)(2,1)} %collective-permute-done.refs_1_), channel_id=1, source_target_pairs={{0,448},{64,0},{128,64},{192,128},{256,192},{320,256},{384,320},{4... | collective-permute-start | bytes 1572872 | tf_op jit(solution)/shard_map/ppermute | solution.py:215
  58.4 8.4 %collective-permute-done.1.refs_2_ = bf16[4,16,8,512]{3,2,1,0:T(8,128)(2,1)S(1)} collective-permute-done((bf16[4,16,8,512]{3,2,1,0:T(8,128)(2,1)}, bf16[4,16,8,512]{3,2,1,0:T(8,128)(2,1)S(1)}, u32[]{:S(2)}, u32[]{:S(2)}) %collective-permute-start.1) | collective-permute-done | bytes 524320 | tf_op jit(solution)/shard_map/ppermute | solution.py:215
  66.8 1.9 %collective-permute-start.3 = (bf16[2,16,8,512]{3,2,1,0:T(8,128)(2,1)S(1)}, bf16[2,16,8,512]{3,2,1,0:T(8,128)(2,1)S(1)}, u32[]{:S(2)}, u32[]{:S(2)}) collective-permute-start(bf16[2,16,8,512]{3,2,1,0:T(8,128)(2,1)S(1)} %slice.8), channel_id=1, source_target_pairs={{0,64},{64,128},{128,192},{192,256},{256,320},{320,384},{384,448},... | collective-permute-start | bytes 786440 | tf_op jit(solution)/shard_map/ppermute | solution.py:215
  68.7 0.0 collective-permute-done.2.refs_3_
  68.8 15.3 %collective-permute-start.4 = (bf16[2,16,8,512]{3,2,1,0:T(8,128)(2,1)S(1)}, bf16[2,16,8,512]{3,2,1,0:T(8,128)(2,1)S(1)}, u32[]{:S(2)}, u32[]{:S(2)}) collective-permute-start(bf16[2,16,8,512]{3,2,1,0:T(8,128)(2,1)S(1)} %slice.9), channel_id=1, source_target_pairs={{0,448},{64,0},{128,64},{192,128},{256,192},{320,256},{384,320},{4... | collective-permute-start | bytes 786440 | tf_op jit(solution)/shard_map/ppermute | solution.py:215
  84.0 3.6 %collective-permute-start.5 = (bf16[4,16,8,512]{3,2,1,0:T(8,128)(2,1)}, bf16[4,16,8,512]{3,2,1,0:T(8,128)(2,1)}, u32[]{:S(2)}, u32[]{:S(2)}) collective-permute-start(bf16[4,16,8,512]{3,2,1,0:T(8,128)(2,1)} %collective-permute-done.refs_1_), channel_id=1, source_target_pairs={{0,16},{16,0},{1,17},{17,1},{2,18},{18,2},{3,19},{19,3},{4,20},{20... | collective-permute-start | bytes 1572872 | tf_op jit(solution)/shard_map/ppermute | solution.py:215
  87.6 1.9 %collective-permute-start.6 = (bf16[4,16,8,512]{3,2,1,0:T(8,128)(2,1)S(1)}, bf16[4,16,8,512]{3,2,1,0:T(8,128)(2,1)}, u32[]{:S(2)}, u32[]{:S(2)}) collective-permute-start(bf16[4,16,8,512]{3,2,1,0:T(8,128)(2,1)S(1)} %collective-permute-done.1.refs_2_), channel_id=1, source_target_pairs={{0,16},{16,0},{1,17},{17,1},{2,18},{18,2},{3,19},{19,3},{4,20},{20... | collective-permute-start | bytes 1572872 | tf_op jit(solution)/shard_map/ppermute | solution.py:215
  89.5 2.4 %collective-permute-start.7 = (bf16[4,16,8,512]{3,2,1,0:T(8,128)(2,1)S(1)}, bf16[4,16,8,512]{3,2,1,0:T(8,128)(2,1)}, u32[]{:S(2)}, u32[]{:S(2)}) collective-permute-start(bf16[4,16,8,512]{3,2,1,0:T(8,128)(2,1)S(1)} %collective-permute-done.2.refs_3_), channel_id=1, source_target_pairs={{0,16},{16,0},{1,17},{17,1},{2,18},{18,2},{3,19},{19,3},{4,20},{20... | collective-permute-start | bytes 1572872 | tf_op jit(solution)/shard_map/ppermute | solution.py:215
  92.0 0.0 collective-permute-done.3
  92.0 0.7 constant_dynamic-update-slice_fusion.1
  92.7 0.0 collective-permute-done.4
  92.7 0.7 constant_dynamic-update-slice_fusion.refs_4_
  93.4 1.9 %collective-permute-start.8 = (bf16[4,16,8,512]{3,2,1,0:T(8,128)(2,1)}, bf16[4,16,8,512]{3,2,1,0:T(8,128)(2,1)}, u32[]{:S(2)}, u32[]{:S(2)}) collective-permute-start(bf16[4,16,8,512]{3,2,1,0:T(8,128)(2,1)} %constant_dynamic-update-slice_fusion.refs_4_), channel_id=1, source_target_pairs={{0,16},{16,0},{1,17},{17,1},{2,18},{18,2},{3,19},{19,3},{4,20},{20... | collective-permute-start | bytes 1572872 | tf_op jit(solution)/shard_map/ppermute | solution.py:215
  95.3 0.7 dynamic-slice_bitcast_fusion.place_ref
  96.0 0.0 collective-permute-done.5.refs_5_
  96.1 1.5 %collective-permute-done.8.refs_8_ = bf16[4,16,8,512]{3,2,1,0:T(8,128)(2,1)} collective-permute-done((bf16[4,16,8,512]{3,2,1,0:T(8,128)(2,1)}, bf16[4,16,8,512]{3,2,1,0:T(8,128)(2,1)}, u32[]{:S(2)}, u32[]{:S(2)}) %collective-permute-start.8) | collective-permute-done | bytes 524320 | tf_op jit(solution)/shard_map/ppermute | solution.py:215
  97.6 4.0 %cross.1 = bf16[2,16,128,256]{3,2,1,0:T(8,128)(2,1)} custom-call(s32[12]{0:T(128)S(1)} %dynamic-slice_bitcast_fusion.place_ref, bf16[16,16,8,512]{3,2,1,0:T(8,128)(2,1)S(1)} %bitcast.5, bf16[4,16,8,512]{3,2,1,0:T(8,128)(2,1)} %collective-permute-done.refs_1_, bf16[4,16,8,512]{3,2,1,0:T(8,128)(2,1)S(1)} %collective-permute-done.1.refs_2_, ...), custom_call_target="tpu_custom_call" | custom-call | flops 1100000000 | bytes 8388608 | tf_op jit(solution)/shard_map/cross/pallas_call | solution.py:155
  (5 shorter events, 0.0 us)
Async XLA Ops:
  18.1 14.9 %collective-permute-start = (bf16[4,16,8,512]{3,2,1,0:T(8,128)(2,1)S(1)}, bf16[4,16,8,512]{3,2,1,0:T(8,128)(2,1)}, u32[]{:S(2)}, u32[]{:S(2)}) collective-permute-start(bf16[4,16,8,512]{3,2,1,0:T(8,128)(2,1)S(1)} %bitcast.6), channel_id=1, source_target_pairs={{0,0},{16,16},{1,256},{17,272},{2,32},{18,48},{3,288},{19,304},{4,... | collective-permute-start | bytes 1572872 | tf_op jit(solution)/shard_map/ppermute | solution.py:242
  23.7 72.4 %all-to-all-start = ((bf16[4,4,16,8,512]{4,3,2,1,0:T(8,128)(2,1)}), bf16[4,4,16,8,512]{4,3,2,1,0:T(8,128)(2,1)S(1)}, u32[]{:S(2)}, u32[]{:S(2)}) async-start(bf16[4,4,16,8,512]{4,3,2,1,0:T(8,128)(2,1)} %broadcast_in_dim.2), calls=%async_computation | async-start | bytes 4194304 | tf_op jit(solution)/shard_map/all_to_all | solution.py:243
  32.9 33.8 %collective-permute-start.1 = (bf16[4,16,8,512]{3,2,1,0:T(8,128)(2,1)}, bf16[4,16,8,512]{3,2,1,0:T(8,128)(2,1)S(1)}, u32[]{:S(2)}, u32[]{:S(2)}) collective-permute-start(bf16[4,16,8,512]{3,2,1,0:T(8,128)(2,1)} %collective-permute-done.refs_1_), channel_id=1, source_target_pairs={{0,64},{64,128},{128,192},{192,256},{256,320},{320,384},{384,448},... | collective-permute-start | bytes 1572872 | tf_op jit(solution)/shard_map/ppermute | solution.py:215
  36.9 31.8 %collective-permute-start.2 = (bf16[4,16,8,512]{3,2,1,0:T(8,128)(2,1)}, bf16[4,16,8,512]{3,2,1,0:T(8,128)(2,1)S(1)}, u32[]{:S(2)}, u32[]{:S(2)}) collective-permute-start(bf16[4,16,8,512]{3,2,1,0:T(8,128)(2,1)} %collective-permute-done.refs_1_), channel_id=1, source_target_pairs={{0,448},{64,0},{128,64},{192,128},{256,192},{320,256},{384,320},{4... | collective-permute-start | bytes 1572872 | tf_op jit(solution)/shard_map/ppermute | solution.py:215
  66.8 25.2 %collective-permute-start.3 = (bf16[2,16,8,512]{3,2,1,0:T(8,128)(2,1)S(1)}, bf16[2,16,8,512]{3,2,1,0:T(8,128)(2,1)S(1)}, u32[]{:S(2)}, u32[]{:S(2)}) collective-permute-start(bf16[2,16,8,512]{3,2,1,0:T(8,128)(2,1)S(1)} %slice.8), channel_id=1, source_target_pairs={{0,64},{64,128},{128,192},{192,256},{256,320},{320,384},{384,448},... | collective-permute-start | bytes 786440 | tf_op jit(solution)/shard_map/ppermute | solution.py:215
  68.8 23.9 %collective-permute-start.4 = (bf16[2,16,8,512]{3,2,1,0:T(8,128)(2,1)S(1)}, bf16[2,16,8,512]{3,2,1,0:T(8,128)(2,1)S(1)}, u32[]{:S(2)}, u32[]{:S(2)}) collective-permute-start(bf16[2,16,8,512]{3,2,1,0:T(8,128)(2,1)S(1)} %slice.9), channel_id=1, source_target_pairs={{0,448},{64,0},{128,64},{192,128},{256,192},{320,256},{384,320},{4... | collective-permute-start | bytes 786440 | tf_op jit(solution)/shard_map/ppermute | solution.py:215
  84.0 12.0 %collective-permute-start.5 = (bf16[4,16,8,512]{3,2,1,0:T(8,128)(2,1)}, bf16[4,16,8,512]{3,2,1,0:T(8,128)(2,1)}, u32[]{:S(2)}, u32[]{:S(2)}) collective-permute-start(bf16[4,16,8,512]{3,2,1,0:T(8,128)(2,1)} %collective-permute-done.refs_1_), channel_id=1, source_target_pairs={{0,16},{16,0},{1,17},{17,1},{2,18},{18,2},{3,19},{19,3},{4,20},{20... | collective-permute-start | bytes 1572872 | tf_op jit(solution)/shard_map/ppermute | solution.py:215
  87.6 8.4 %collective-permute-start.6 = (bf16[4,16,8,512]{3,2,1,0:T(8,128)(2,1)S(1)}, bf16[4,16,8,512]{3,2,1,0:T(8,128)(2,1)}, u32[]{:S(2)}, u32[]{:S(2)}) collective-permute-start(bf16[4,16,8,512]{3,2,1,0:T(8,128)(2,1)S(1)} %collective-permute-done.1.refs_2_), channel_id=1, source_target_pairs={{0,16},{16,0},{1,17},{17,1},{2,18},{18,2},{3,19},{19,3},{4,20},{20... | collective-permute-start | bytes 1572872 | tf_op jit(solution)/shard_map/ppermute | solution.py:215
  89.5 6.5 %collective-permute-start.7 = (bf16[4,16,8,512]{3,2,1,0:T(8,128)(2,1)S(1)}, bf16[4,16,8,512]{3,2,1,0:T(8,128)(2,1)}, u32[]{:S(2)}, u32[]{:S(2)}) collective-permute-start(bf16[4,16,8,512]{3,2,1,0:T(8,128)(2,1)S(1)} %collective-permute-done.2.refs_3_), channel_id=1, source_target_pairs={{0,16},{16,0},{1,17},{17,1},{2,18},{18,2},{3,19},{19,3},{4,20},{20... | collective-permute-start | bytes 1572872 | tf_op jit(solution)/shard_map/ppermute | solution.py:215
  93.4 4.1 %collective-permute-start.8 = (bf16[4,16,8,512]{3,2,1,0:T(8,128)(2,1)}, bf16[4,16,8,512]{3,2,1,0:T(8,128)(2,1)}, u32[]{:S(2)}, u32[]{:S(2)}) collective-permute-start(bf16[4,16,8,512]{3,2,1,0:T(8,128)(2,1)} %constant_dynamic-update-slice_fusion.refs_4_), channel_id=1, source_target_pairs={{0,16},{16,0},{1,17},{17,1},{2,18},{18,2},{3,19},{19,3},{4,20},{20... | collective-permute-start | bytes 1572872 | tf_op jit(solution)/shard_map/ppermute | solution.py:215
